TPU v7x, 32 devices: a whole 2x2x4 slice. The times are simulated.
32 devices in a mesh: slab: 16 (over z, y, core), sub: 2 (over x).
Axes of the slice: x: 2, y: 2, z: 4, core: 2. Of those that a mesh axis runs over, the one named last changes fastest.
Arguments:
- features: bfloat16 [32768, 128], P(('slab', 'sub')), may hold values from -6 to 6
- positions: float32 [3, 32768], P(None, ('slab', 'sub')), may hold values from 0 to 1, as said below
- atom_count: int32 [32], P(('slab', 'sub')), may hold values from 512 to 1024, as said below
- kgrid: int32 [3, 2048], replicated, may hold values from -6 to 6
- k_filter: float32 [2048, 128], replicated, may hold values from 0.1 to 1
- w_mix: float32 [128, 128], replicated, may hold values from -0.5 to 0.5
- w_recv: bfloat16 [128, 128], replicated, may hold values from -0.5 to 0.5
- w_send: bfloat16 [128, 128], replicated, may hold values from -0.5 to 0.5
- w_basis: bfloat16 [8, 128], replicated, may hold values from -2 to 2
- w_out: bfloat16 [128, 128], replicated, may hold values from -0.5 to 0.5
- edge_basis: bfloat16 [8, 1048576], P(None, ('slab', 'sub')), may hold values from -1 to 1
- senders: int32 [1048576], P(('slab', 'sub')), may hold values from 0 to 9215, as said below
Outputs:
- updated: float32 [32768, 128], P(('slab', 'sub'))
Inputs may be any that keep to these rules, and one draw needn't show every extreme that they name: `atom_count`: one block has exactly 1024 live atoms; live atoms of a block are its first rows. senders[e] = (3 a + c) * 1024 + j with a, c in 0..2 and j below the atom_count of the block it names. Each atom of block (s, b) has positions[0] in [b / 2, (b + 1) / 2), positions[2] in [s / 16, (s + 1) / 16), positions[1] in [0, 1).
All inputs are finite; a program needn't handle non-finite values.
Results may differ from a plain program's by a relative error of at most 0.0021.
Values may be sent and summed in bfloat16 or wider, within the bound.
A program may use at most 128 MiB of HBM per device.

v0:
```python
import math

import jax
import jax.numpy as jnp
from jax import lax
from jax.sharding import PartitionSpec as P


def extended(cells, sides, width):
    for axis, dim in sides:
        count = lax.axis_size(axis)
        head = lax.slice_in_dim(cells, 0, width, axis=dim)
        tail = lax.slice_in_dim(cells, cells.shape[dim] - width, cells.shape[dim], axis=dim)
        cells = jnp.concatenate(
            [
                lax.ppermute(tail, axis, [(i, (i + 1) % count) for i in range(count)]),
                cells,
                lax.ppermute(head, axis, [((i + 1) % count, i) for i in range(count)]),
            ],
            axis=dim,
        )
    return cells


def phase_tables(k_rows, coords):
    wave = k_rows.astype(jnp.float32)
    phase = (
        wave[0][:, None] * coords[0][None, :]
        + wave[1][:, None] * coords[1][None, :]
        + wave[2][:, None] * coords[2][None, :]
    ) * (2.0 * math.pi)
    return (jnp.cos(phase).astype(jnp.bfloat16), jnp.sin(phase).astype(jnp.bfloat16))


def whole_tables(kgrid, coords):
    k_count = kgrid.shape[1]
    k_step = 512
    blocks = kgrid.reshape(3, k_count // k_step, k_step).transpose(1, 0, 2)
    cos_parts, sin_parts = lax.map(lambda wave: phase_tables(wave, coords), blocks)
    atom_rows = coords.shape[1]
    return (cos_parts.reshape(k_count, atom_rows), sin_parts.reshape(k_count, atom_rows))


def filter_rows(factor_sums, k_filter, w_mix, norm_factor):
    channels = k_filter.shape[1]
    real_part = jnp.dot(
        factor_sums[:, :channels] * norm_factor * k_filter,
        w_mix,
        precision=lax.Precision.HIGHEST,
        preferred_element_type=jnp.float32,
    )
    imag_part = jnp.dot(
        factor_sums[:, channels:] * norm_factor * k_filter,
        w_mix,
        precision=lax.Precision.HIGHEST,
        preferred_element_type=jnp.float32,
    )
    return jnp.concatenate([real_part, imag_part], axis=1).astype(jnp.bfloat16)


def edge_messages(recv_proj, sender_pool, senders, edge_basis, w_basis, w_out, degree):
    atom_rows = recv_proj.shape[0]
    channels = recv_proj.shape[1]
    gathered = (
        jnp.take(sender_pool, senders, axis=0)
        .astype(jnp.float32)
        .reshape(atom_rows, degree, channels)
    )
    radial = lax.dot_general(
        edge_basis, w_basis, (((0,), (0,)), ((), ())), preferred_element_type=jnp.float32
    ).reshape(atom_rows, degree, channels)
    hidden = jax.nn.silu(recv_proj[:, None, :] + gathered + radial).astype(jnp.bfloat16)
    message = jnp.dot(
        hidden.reshape(atom_rows * degree, channels), w_out, preferred_element_type=jnp.float32
    )
    return jnp.sum(message.reshape(atom_rows, degree, channels), axis=1) * (1.0 / math.sqrt(degree))


def per_device(
    features,
    positions,
    atom_count,
    kgrid,
    k_filter,
    w_mix,
    w_recv,
    w_send,
    w_basis,
    w_out,
    edge_basis,
    senders,
):
    atom_rows, channels = features.shape
    degree = senders.shape[0] // atom_rows
    total_k = kgrid.shape[1]
    devices = lax.axis_size(("slab", "sub"))
    norm_factor = 1.0 / math.sqrt(atom_rows * devices)
    live_mask = (jnp.arange(atom_rows, dtype=jnp.int32) < atom_count[0]).astype(jnp.float32)
    masked = (features.astype(jnp.float32) * live_mask[:, None]).astype(jnp.bfloat16)
    ghost_grid = extended(
        features.reshape(1, 1, atom_rows * channels), (("slab", 0), ("sub", 1)), 1
    )
    sender_pool = jnp.dot(
        ghost_grid.reshape(9 * atom_rows, channels), w_send, preferred_element_type=jnp.float32
    ).astype(jnp.bfloat16)
    cos_table, sin_table = whole_tables(kgrid, positions)
    k_share = total_k // devices
    cos_rows = cos_table
    sin_rows = sin_table
    owned = lax.psum_scatter(
        jnp.concatenate(
            [
                jnp.dot(cos_rows, masked, preferred_element_type=jnp.float32),
                jnp.dot(sin_rows, masked, preferred_element_type=jnp.float32),
            ],
            axis=1,
        ),
        ("slab", "sub"),
        scatter_dimension=0,
        tiled=True,
    )
    k_first = lax.axis_index(("slab", "sub")) * k_share
    filtered = filter_rows(
        owned, lax.dynamic_slice_in_dim(k_filter, k_first, k_share, 0), w_mix, norm_factor
    )
    block_rows = lax.all_gather(filtered, ("slab", "sub"), axis=0, tiled=True)
    cos_rows = cos_table
    sin_rows = sin_table
    contract = (((0,), (0,)), ((), ()))
    first_term = lax.dot_general(
        cos_rows, block_rows[:, :channels], contract, preferred_element_type=jnp.float32
    )
    second_term = lax.dot_general(
        sin_rows, block_rows[:, channels:], contract, preferred_element_type=jnp.float32
    )
    long_range = first_term + second_term
    recv_proj = jnp.dot(features, w_recv, preferred_element_type=jnp.float32)
    aggregate = edge_messages(recv_proj, sender_pool, senders, edge_basis, w_basis, w_out, degree)
    return live_mask[:, None] * (aggregate + long_range * (4.0 / math.sqrt(total_k)))


def solution(mesh):
    placed = (
        P(("slab", "sub"), None),
        P(None, ("slab", "sub")),
        P(("slab", "sub")),
        P(),
        P(),
        P(),
        P(),
        P(),
        P(),
        P(),
        P(None, ("slab", "sub")),
        P(("slab", "sub")),
    )
    return jax.shard_map(
        per_device, mesh=mesh, in_specs=placed, out_specs=P(("slab", "sub"), None), check_vma=False
    )
```

profile of v0, /device:TPU:0, one launch (start us, length us, event | category | flops | bytes accessed | tf_op | source)
XLA Modules:
  0.0 354.4 jit_solution(15435289275248292483)
XLA Ops:
  6.5 0.0 copy-start
  6.5 0.0 reduce-scatter.4.cloned.1.call-start
  6.5 1.9 reshape.367
  8.5 5.4 %collective-permute-start.1 = (bf16[1,1,131072]{2,0,1:T(2,128)(2,1)}, bf16[1,1,131072]{2,0,1:T(2,128)(2,1)}, u32[]{:S(2)}, u32[]{:S(2)}) collective-permute-start(bf16[1,1,131072]{2,0,1:T(2,128)(2,1)} %reshape.367), channel_id=1, source_target_pairs={{2,0},{4,2},{6,4},{8,6},{10,8},{12,10},{14,12},{16,14},{18,16},{20... | collective-permute-start | bytes 786440 | tf_op jit(solution)/shard_map/ppermute | solution.py:18
  13.9 0.0 collective-permute-start
  14.6 0.0 copy-start.4
  14.6 44.7 %while.12 = (s32[]{:T(128)}, bf16[4,512,1024]{2,1,0:T(8,128)(2,1)}, bf16[4,512,1024]{2,1,0:T(8,128)(2,1)}, s32[4,3,512]{2,1,0:T(4,128)}, f32[3,1024]{1,0:T(4,128)}, /*index=5*/s32[]{:T(128)}) while((s32[]{:T(128)}, bf16[4,512,1024]{2,1,0:T(8,128)(2,1)}, bf16[4,512,1024]{2,1,0:T(8,128)(2,1)}, s32[4,3,512]{2,1,0:T(4,128)}, f32[3,1024]{1,0:T(4,128)}, ...), condition=%wide.region_2.3_spmd, body=%wide.region_1.2_spmd.sunk | while | flops 4195842 | bytes 2164821 | solution.py:39
  14.6 0.7 dynamic-slice_convert_fusion.2
  15.4 0.8 fusion.45
  16.2 9.6 %fusion.47 = (bf16[4,512,1024]{2,1,0:T(8,128)(2,1)}, bf16[4,512,1024]{2,1,0:T(8,128)(2,1)}) fusion(bf16[4,512,1024]{2,1,0:T(8,128)(2,1)} %get-tuple-element.110, s32[]{:T(128)S(6)} %copy.34, f32[1024]{0:T(1024)S(1)} %bitcast.49, f32[512]{0:T(512)S(1)} %bitcast.52, f32[1024]{0:T(1024)S(1)} %bitcast.50, f32[512]{0:T(512)S(1)} %bitcast.53, ...), kind=kLoop, calls=%fused_computation.5.clone.1 | loop fusion | flops 4194304 | bytes 2115588 | tf_op jit(solution)/shard_map/while/body/jit(dynamic_update_index_in_dim)/dynamic_update_slice | solution.py:39
  25.8 0.7 dynamic-slice_convert_fusion.2
  26.5 0.8 fusion.45
  27.4 9.6 %fusion.47 = (bf16[4,512,1024]{2,1,0:T(8,128)(2,1)}, bf16[4,512,1024]{2,1,0:T(8,128)(2,1)}) fusion(bf16[4,512,1024]{2,1,0:T(8,128)(2,1)} %get-tuple-element.110, s32[]{:T(128)S(6)} %copy.34, f32[1024]{0:T(1024)S(1)} %bitcast.49, f32[512]{0:T(512)S(1)} %bitcast.52, f32[1024]{0:T(1024)S(1)} %bitcast.50, f32[512]{0:T(512)S(1)} %bitcast.53, ...), kind=kLoop, calls=%fused_computation.5.clone.1 | loop fusion | flops 4194304 | bytes 2115588 | tf_op jit(solution)/shard_map/while/body/jit(dynamic_update_index_in_dim)/dynamic_update_slice | solution.py:39
  37.0 0.7 dynamic-slice_convert_fusion.2
  37.7 0.8 fusion.45
  38.5 9.6 %fusion.47 = (bf16[4,512,1024]{2,1,0:T(8,128)(2,1)}, bf16[4,512,1024]{2,1,0:T(8,128)(2,1)}) fusion(bf16[4,512,1024]{2,1,0:T(8,128)(2,1)} %get-tuple-element.110, s32[]{:T(128)S(6)} %copy.34, f32[1024]{0:T(1024)S(1)} %bitcast.49, f32[512]{0:T(512)S(1)} %bitcast.52, f32[1024]{0:T(1024)S(1)} %bitcast.50, f32[512]{0:T(512)S(1)} %bitcast.53, ...), kind=kLoop, calls=%fused_computation.5.clone.1 | loop fusion | flops 4194304 | bytes 2115588 | tf_op jit(solution)/shard_map/while/body/jit(dynamic_update_index_in_dim)/dynamic_update_slice | solution.py:39
  48.1 0.7 dynamic-slice_convert_fusion.2
  48.8 0.8 fusion.45
  49.7 9.6 %fusion.47 = (bf16[4,512,1024]{2,1,0:T(8,128)(2,1)}, bf16[4,512,1024]{2,1,0:T(8,128)(2,1)}) fusion(bf16[4,512,1024]{2,1,0:T(8,128)(2,1)} %get-tuple-element.110, s32[]{:T(128)S(6)} %copy.34, f32[1024]{0:T(1024)S(1)} %bitcast.49, f32[512]{0:T(512)S(1)} %bitcast.52, f32[1024]{0:T(1024)S(1)} %bitcast.50, f32[512]{0:T(512)S(1)} %bitcast.53, ...), kind=kLoop, calls=%fused_computation.5.clone.1 | loop fusion | flops 4194304 | bytes 2115588 | tf_op jit(solution)/shard_map/while/body/jit(dynamic_update_index_in_dim)/dynamic_update_slice | solution.py:39
  59.3 0.0 copy-done.4
  59.3 3.9 %fusion.15 = f32[2048,128]{0,1:T(8,128)S(1)} fusion(bf16[2048,1024]{1,0:T(8,128)(2,1)} %bitcast.46, bf16[1024,128]{1,0:T(8,128)(2,1)S(1)} %copy-done.4, f32[1024]{0:T(1024)S(1)} %fusion.23), kind=kOutput, calls=%fused_computation.31 | convolution fusion | flops 537264128 | bytes 5509120 | tf_op jit(solution)/shard_map/dot_general | solution.py:113
  63.2 0.0 copy-done.2
  63.2 1.6 fusion.14
  64.8 0.1 pad_maximum_fusion.1
  65.0 1.8 copy.20
  66.8 0.0 reduce-scatter.4.cloned.1.call-update
  66.8 0.0 all-gather.2.cloned.1.call-start
  66.9 0.9 fusion.13
  67.8 0.0 copy-done
  67.9 0.1 copy.23
  68.0 1.0 fusion.29
  68.9 0.0 collective-permute-done.1
  68.9 0.0 collective-permute-done
  69.0 3.2 pad_maximum_fusion.2
  72.1 1.6 collective-permute-start.3
  73.7 0.5 collective-permute-start.2
  74.2 0.0 copy-done.5
  74.3 36.1 %collective-permute-done.3 = bf16[3,1,131072]{2,0,1:T(4,128)(2,1)S(1)} collective-permute-done((bf16[3,1,131072]{2,0,1:T(4,128)(2,1)S(1)}, bf16[3,1,131072]{2,0,1:T(4,128)(2,1)S(1)}, u32[]{:S(2)}, u32[]{:S(2)}) %collective-permute-start.3) | collective-permute-done | bytes 786464 | tf_op jit(solution)/shard_map/ppermute | solution.py:18
  110.3 29.1 %collective-permute-done.2 = bf16[3,1,131072]{2,0,1:T(4,128)(2,1)S(1)} collective-permute-done((bf16[3,1,131072]{2,0,1:T(4,128)(2,1)S(1)}, bf16[3,1,131072]{2,0,1:T(4,128)(2,1)S(1)}, u32[]{:S(2)}, u32[]{:S(2)}) %collective-permute-start.2) | collective-permute-done | bytes 786464 | tf_op jit(solution)/shard_map/ppermute | solution.py:16
  139.5 4.1 %pad_maximum_fusion = bf16[3,3,131072]{2,0,1:T(4,128)(2,1)S(1)} fusion(bf16[3,1,131072]{2,0,1:T(4,128)(2,1)S(1)} %collective-permute-done.3, bf16[1,1,131072]{2,0,1:T(2,128)(2,1)} %collective-permute-done.1, bf16[1,1,131072]{2,0,1:T(2,128)(2,1)} %reshape.367, bf16[1,1,131072]{2,0,1:T(2,128)(2,1)} %collective-permute-done, ...), kind=kLoop, calls=%fused_computation.14 | loop fusion | flops 11796480 | bytes 4718592 | tf_op jit(solution)/shard_map/concatenate | solution.py:14
  143.6 4.1 %copy.17 = bf16[3,3,131072]{2,1,0:T(4,128)(2,1)} copy(bf16[3,3,131072]{2,0,1:T(4,128)(2,1)S(1)} %pad_maximum_fusion) | data formatting | bytes 4718592 | tf_op jit(solution)/shard_map/concatenate | solution.py:14
  147.7 5.8 %reshape.368 = bf16[9216,128]{1,0:T(8,128)(2,1)} reshape(bf16[3,3,131072]{2,1,0:T(4,128)(2,1)} %copy.17) | data formatting | bytes 4718592 | tf_op jit(solution)/shard_map/reshape | solution.py:104
  153.4 0.0 copy-done.8
  153.4 2.4 convolution_convert_fusion
  155.9 114.2 %gather_fusion = bf16[32768,128]{1,0:T(8,128)(2,1)} fusion(bf16[9216,128]{1,0:T(8,128)(2,1)S(1)} %convolution_convert_fusion, s32[32768]{0:T(1024)S(1)} %fusion.13), kind=kCustom, calls=%fused_computation | custom fusion | bytes 16908288 | tf_op jit(solution)/shard_map/jit(_take)/gather | solution.py:65
  270.0 9.1 %bitcast_add_fusion = f32[32768,128]{1,0:T(8,128)} fusion(bf16[32768,128]{1,0:T(8,128)(2,1)} %gather_fusion, f32[1024,128]{1,0:T(8,128)S(1)} %fusion.29, pred[32768]{0:T(1024)(128)(4,1)S(1)} %compare_and_fusion), kind=kLoop, calls=%fused_computation.8 | loop fusion | flops 12582912 | bytes 25722880 | tf_op jit(solution)/shard_map/add | solution.py:72
  279.1 0.8 fusion.28
  279.9 0.1 copy.22
  280.0 0.1 copy.24
  280.1 0.0 copy-done.7
  280.1 0.3 convolution_convert_fusion.2
  280.4 0.3 convolution_convert_fusion.1
  280.7 0.6 pad_maximum_fusion.3
  281.3 0.0 all-gather.2.cloned.1.call-update
  281.3 0.0 copy-done.9
  281.3 0.0 copy-start.10
  281.3 8.7 %multiply_convert_fusion = bf16[32768,128]{1,0:T(8,128)(2,1)S(1)} fusion(f32[32768,128]{1,0:T(8,128)} %bitcast_add_fusion, bf16[8,32768]{1,0:T(8,128)(2,1)S(1)} %copy-done.9, bf16[8,128]{1,0:T(8,128)(2,1)S(1)} %copy-done.11), kind=kOutput, calls=%fused_computation.9 | convolution fusion | flops 92274688 | bytes 25692160 | tf_op jit(solution)/shard_map/dot_general | solution.py:69
  290.1 5.1 %fusion.4 = f32[1024,128]{1,0:T(8,128)S(1)} fusion(bf16[1024,32,128]{2,1,0:T(8,128)(2,1)S(1)} %bitcast.55, bf16[128,128]{1,0:T(8,128)(2,1)S(1)} %copy-done.10), kind=kOutput, calls=%fused_computation.13 | convolution fusion | flops 1077805056 | bytes 8945664 | tf_op jit(solution)/shard_map/dot_general | solution.py:73
  295.3 46.2 %all-gather.2.cloned.1.call-done = bf16[2048,256]{1,0:T(8,128)(2,1)} async-done(((bf16[64,256]{1,0:T(8,128)(2,1)}), bf16[2048,256]{1,0:T(8,128)(2,1)}) %all-gather.2.cloned.1.call-update) | async-done | bytes 1048592 | tf_op jit(solution)/shard_map/all_gather | solution.py:126
  341.5 3.7 %fusion.11 = f32[1024,128]{1,0:T(8,128)S(1)} fusion(bf16[2048,1024]{1,0:T(8,128)(2,1)} %bitcast.47, bf16[2048,256]{1,0:T(8,128)(2,1)} %all-gather.2.cloned.1.call-done), kind=kOutput, calls=%fused_computation.24 | convolution fusion | flops 536870912 | bytes 5242880 | tf_op jit(solution)/shard_map/dot_general | solution.py:130
  345.2 0.0 copy-done.3
  345.2 0.2 copy-done.6
  345.4 2.2 fusion.9
  347.6 0.0 copy-done.1
  (21 shorter events, 0.1 us)
Async XLA Ops:
  6.5 61.3 %copy-start = (f32[2048,128]{1,0:T(8,128)S(1)}, f32[2048,128]{1,0:T(8,128)}, u32[]{:S(2)}) copy-start(f32[2048,128]{1,0:T(8,128)} %param.18) | copy-start | bytes 3145732
  6.5 272.6 %reduce-scatter.4.cloned.1.call-start = ((), (), s32[]{:S(2)}) async-start(), calls=%async_computation.2 | async-start | bytes 2162688
  8.5 60.5 %collective-permute-start.1 = (bf16[1,1,131072]{2,0,1:T(2,128)(2,1)}, bf16[1,1,131072]{2,0,1:T(2,128)(2,1)}, u32[]{:S(2)}, u32[]{:S(2)}) collective-permute-start(bf16[1,1,131072]{2,0,1:T(2,128)(2,1)} %reshape.367), channel_id=1, source_target_pairs={{2,0},{4,2},{6,4},{8,6},{10,8},{12,10},{14,12},{16,14},{18,16},{20... | collective-permute-start | bytes 786440 | tf_op jit(solution)/shard_map/ppermute | solution.py:18
  13.9 55.0 %collective-permute-start = (bf16[1,1,131072]{2,0,1:T(2,128)(2,1)}, bf16[1,1,131072]{2,0,1:T(2,128)(2,1)}, u32[]{:S(2)}, u32[]{:S(2)}) collective-permute-start(bf16[1,1,131072]{2,0,1:T(2,128)(2,1)} %reshape.367), channel_id=1, source_target_pairs={{0,2},{2,4},{4,6},{6,8},{8,10},{10,12},{12,14},{14,16},{16,18},{18... | collective-permute-start | bytes 786440 | tf_op jit(solution)/shard_map/ppermute | solution.py:16
  14.6 44.7 %copy-start.4 = (bf16[1024,128]{1,0:T(8,128)(2,1)S(1)}, bf16[1024,128]{1,0:T(8,128)(2,1)}, u32[]{:S(2)}) copy-start(bf16[1024,128]{1,0:T(8,128)(2,1)} %param.14) | copy-start | bytes 786436
  59.3 3.9 %copy-start.2 = (bf16[4,512,1024]{2,1,0:T(8,128)(2,1)S(1)}, bf16[4,512,1024]{2,1,0:T(8,128)(2,1)}, u32[]{:S(2)}) copy-start(bf16[4,512,1024]{2,1,0:T(8,128)(2,1)} %get-tuple-element.34) | copy-start | bytes 12582916
  66.8 7.4 %copy-start.5 = (s32[32768]{0:T(1024)S(1)}, s32[32768]{0:T(1024)}, u32[]{:S(2)}) copy-start(s32[32768]{0:T(1024)} %param.25) | copy-start | bytes 393220
  66.8 274.7 %all-gather.2.cloned.1.call-start = ((), (), s32[]{:S(2)}) async-start(), calls=%async_computation.1 | async-start | bytes 1081344 | tf_op jit(solution)/shard_map/all_gather | solution.py:126
  72.1 38.2 %collective-permute-start.3 = (bf16[3,1,131072]{2,0,1:T(4,128)(2,1)S(1)}, bf16[3,1,131072]{2,0,1:T(4,128)(2,1)S(1)}, u32[]{:S(2)}, u32[]{:S(2)}) collective-permute-start(bf16[3,1,131072]{2,0,1:T(4,128)(2,1)S(1)} %pad_maximum_fusion.2), channel_id=1, source_target_pairs={{1,0},{0,1},{3,2},{2,3},{5,4},{4,5},{7,6},{6,7},{9,8},{8,9},{11,10... | collective-permute-start | bytes 2359304 | tf_op jit(solution)/shard_map/ppermute | solution.py:18
  73.7 65.8 %collective-permute-start.2 = (bf16[3,1,131072]{2,0,1:T(4,128)(2,1)S(1)}, bf16[3,1,131072]{2,0,1:T(4,128)(2,1)S(1)}, u32[]{:S(2)}, u32[]{:S(2)}) collective-permute-start(bf16[3,1,131072]{2,0,1:T(4,128)(2,1)S(1)} %pad_maximum_fusion.2), channel_id=1, source_target_pairs={{0,1},{1,0},{2,3},{3,2},{4,5},{5,4},{6,7},{7,6},{8,9},{9,8},{10,11... | collective-permute-start | bytes 2359304 | tf_op jit(solution)/shard_map/ppermute | solution.py:16
  147.7 5.8 %copy-start.8 = (bf16[128,128]{1,0:T(8,128)(2,1)S(1)}, bf16[128,128]{1,0:T(8,128)(2,1)}, u32[]{:S(2)}) copy-start(bf16[128,128]{1,0:T(8,128)(2,1)} %param.21) | copy-start | bytes 98308
  270.0 10.1 %copy-start.7 = (f32[128,128]{1,0:T(8,128)S(1)}, f32[128,128]{1,0:T(8,128)}, u32[]{:S(2)}) copy-start(f32[128,128]{1,0:T(8,128)} %param.19) | copy-start | bytes 196612
  270.0 11.3 %copy-start.9 = (bf16[8,32768]{1,0:T(8,128)(2,1)S(1)}, bf16[8,32768]{1,0:T(8,128)(2,1)}, u32[]{:S(2)}) copy-start(bf16[8,32768]{1,0:T(8,128)(2,1)} %param.24) | copy-start | bytes 1572868
  270.0 11.3 %copy-start.11 = (bf16[8,128]{1,0:T(8,128)(2,1)S(1)}, bf16[8,128]{1,0:T(8,128)(2,1)}, u32[]{:S(2)}) copy-start(bf16[8,128]{1,0:T(8,128)(2,1)} %param.22) | copy-start | bytes 6148
  281.3 8.8 %copy-start.10 = (bf16[128,128]{1,0:T(8,128)(2,1)S(1)}, bf16[128,128]{1,0:T(8,128)(2,1)}, u32[]{:S(2)}) copy-start(bf16[128,128]{1,0:T(8,128)(2,1)} %param.23) | copy-start | bytes 98308
  341.5 3.7 %copy-start.3 = (bf16[4,512,1024]{2,1,0:T(8,128)(2,1)S(1)}, bf16[4,512,1024]{2,1,0:T(8,128)(2,1)}, u32[]{:S(2)}) copy-start(bf16[4,512,1024]{2,1,0:T(8,128)(2,1)} %get-tuple-element.34) | copy-start | bytes 12582916
  341.5 3.9 %copy-start.6 = (bf16[2048,256]{1,0:T(8,128)(2,1)S(1)}, bf16[2048,256]{1,0:T(8,128)(2,1)}, u32[]{:S(2)}) copy-start(bf16[2048,256]{1,0:T(8,128)(2,1)} %all-gather.2.cloned.1.call-done) | copy-start | bytes 3145732
  341.5 6.1 %copy-start.1 = (f32[2048,128]{1,0:T(8,128)S(1)}, f32[2048,128]{1,0:T(8,128)}, u32[]{:S(2)}) copy-start(f32[2048,128]{1,0:T(8,128)} %param.18) | copy-start | bytes 3145732
Sparse Core Ops, SparseCore 0:
  67.0 139.6 reduce-scatter.3
  281.4 60.0 all-gather.1
where the time goes:
time: 355 us; the launch traced here: 354 us
  local copies, waits for them, and re-layouts  132 us (37%)
  waiting for transfers between devices  111 us (31%)
  other arithmetic  59.4 us (17%)
  matrix products  29.2 us (8%)
  between operations  14.3 us (4%)
  starting transfers between devices  7.58 us (2%)
    gather x1, local copies, waits for them, and re-layouts, edge_messages(): jnp.take(sender_pool, senders, axis=0).astype(jnp.float32)  114 us
    all_gather x1, waiting for transfers between devices, per_device(): block_rows = lax.all_gather(filtered, ('slab', 'sub'), axis=0, tiled=True)  46.2 us
    dynamic_update_slice x4, other arithmetic, whole_tables(): lax.map(lambda wave: phase_tables(wave, coords), blocks)  38.4 us
    ppermute x2, waiting for transfers between devices, extended(): lax.ppermute(head, axis, [((i + 1) % count, i) for i in range(count)])  36.1 us
    ppermute x2, waiting for transfers between devices, extended(): lax.ppermute(tail, axis, [(i, (i + 1) % count) for i in range(count)])  29.1 us
    add x1, other arithmetic, edge_messages(): recv_proj[:, None, :] + gathered + radial  9.09 us
    dot_general x1, matrix products, edge_messages(): lax.dot_general(edge_basis, w_basis, (((0,), (0,)), ((), ())), preferred_...  8.75 us
    concatenate x2, other arithmetic, extended(): jnp.concatenate([lax.ppermute(tail, axis, [(i, (i + 1) % count) for i in...  7.29 us
  transfers between devices with their start and end apart: 6, of which 3 were waited for; matrix products, arithmetic and copies ran while one was open for 60% of the time, Pallas kernels for 0%

commit v1 on v0

v1 whole, which is shorter than its diff:
```python
import math

import jax
import jax.numpy as jnp
from jax import lax
from jax.experimental import pallas as pl
from jax.experimental.pallas import tpu as pltpu
from jax.sharding import PartitionSpec as P

KMAX = 6
SIDE = 2 * KMAX + 1
PAIRS = 96
MIB = 1024 * 1024
CONTRACT_FIRST = (((0,), (0,)), ((), ()))


def table_kernel(base_cos, base_sin, masked_ref, table_ref, sums_ref, pair_cos, pair_sin):
    grid_rows = table_ref.shape[0] // 2
    channels = masked_ref.shape[1]
    atom_rows = masked_ref.shape[0]
    for a in range(KMAX + 1):
        cx, sx = base_cos[a : a + 1, :], base_sin[a : a + 1, :]
        cy, sy = base_cos[16 : 16 + SIDE, :], base_sin[16 : 16 + SIDE, :]
        pair_cos[a * SIDE : (a + 1) * SIDE, :] = cx * cy - sx * sy
        pair_sin[a * SIDE : (a + 1) * SIDE, :] = sx * cy + cx * sy
    used = (KMAX + 1) * SIDE
    pair_cos[used:, :] = jnp.zeros((PAIRS - used, atom_rows), jnp.float32)
    pair_sin[used:, :] = jnp.zeros((PAIRS - used, atom_rows), jnp.float32)

    def one_plane(q, carry):
        cz, sz = base_cos[pl.ds(32 + q, 1), :], base_sin[pl.ds(32 + q, 1), :]
        cosines = (pair_cos[...] * cz - pair_sin[...] * sz).astype(jnp.bfloat16)
        sines = (pair_sin[...] * cz + pair_cos[...] * sz).astype(jnp.bfloat16)
        at = pl.multiple_of(q * PAIRS, PAIRS)
        table_ref[pl.ds(at, PAIRS), :] = cosines
        table_ref[pl.ds(at + grid_rows, PAIRS), :] = sines
        sums_ref[pl.ds(at, PAIRS), :channels] = jnp.dot(
            cosines, masked_ref[...], preferred_element_type=jnp.float32
        )
        sums_ref[pl.ds(at, PAIRS), channels:] = jnp.dot(
            sines, masked_ref[...], preferred_element_type=jnp.float32
        )
        return carry

    lax.fori_loop(0, SIDE, one_plane, 0)
    tail = grid_rows - SIDE * PAIRS
    if tail:
        for start in (SIDE * PAIRS, grid_rows + SIDE * PAIRS):
            table_ref[start : start + tail, :] = jnp.zeros((tail, atom_rows), jnp.bfloat16)
        sums_ref[SIDE * PAIRS :, :] = jnp.zeros((tail, 2 * channels), jnp.float32)


def edge_rows(degree, group, it, snd_ref, pool, basis_ref, w_basis, recv, total):
    edges = group * degree
    first = pl.multiple_of(it * edges, edges)
    row = pl.multiple_of(it * group, group)
    radial = lax.dot_general(
        basis_ref[:, pl.ds(first, edges)],
        w_basis[...],
        CONTRACT_FIRST,
        preferred_element_type=jnp.float32,
    )
    recv_rows = recv[pl.ds(row, group), :]
    sublane = lax.broadcasted_iota(jnp.int32, pool.shape[1:], 0)
    sums = []
    for j in range(group):
        octets = []
        for octet in range(degree // 8):
            start = first + j * degree + octet * 8
            picked = pool[snd_ref[start]]
            for k in range(1, 8):
                picked = jnp.where(sublane == k, pool[snd_ref[start + k]], picked)
            octets.append(picked)
        gathered = jnp.concatenate(octets, axis=0)
        v = gathered + radial[j * degree : (j + 1) * degree, :] + recv_rows[j : j + 1, :]
        half = 0.5 * v
        hidden = (half + half * jnp.tanh(half)).astype(jnp.bfloat16)
        sums.append(jnp.sum(hidden.astype(jnp.float32), axis=0, keepdims=True))
    total[pl.ds(row, group), :] = jnp.concatenate(sums, axis=0)


def fused_kernel(
    plan,
    snd_ref,
    left_ref,
    mid_ref,
    right_ref,
    basis_ref,
    feat_ref,
    w_recv,
    w_basis,
    w_out,
    sums_ref,
    filter_ref,
    w_mix,
    agg_ref,
    factor_ref,
    pool,
    recv,
    total,
    in_plane,
    part,
    in_line,
    line_rows,
    plane_rows,
    send_a,
    recv_a,
    send_b,
    recv_b,
    send_c,
    recv_c,
    send_d,
    recv_d,
):
    degree, cols, low, members, lines, share, norm_factor = plan
    channels = feat_ref.shape[1]
    step = pl.program_id(0)
    slab, sub = lax.axis_index("slab"), lax.axis_index("sub")
    line = slab // low
    member = (slab % low) * cols + sub
    chunk = lines * share

    def plane_peer(r):
        peer = (member + r) % members
        return peer, {"slab": line * low + peer // cols, "sub": peer % cols}

    def line_peer(r):
        peer = (line + r) % lines
        return peer, {"slab": peer * low + slab % low, "sub": sub}

    def copy_a(r):
        peer, where = plane_peer(r)
        rows = pl.ds(pl.multiple_of(peer * chunk, 8), chunk)
        return pltpu.make_async_remote_copy(
            src_ref=sums_ref.at[rows],
            dst_ref=in_plane.at[r - 1],
            send_sem=send_a.at[r - 1],
            recv_sem=recv_a.at[r - 1],
            device_id=where,
            device_id_type=pl.DeviceIdType.MESH,
        )

    def copy_b(r):
        peer, where = line_peer(r)
        rows = pl.ds(pl.multiple_of(peer * share, 8), share)
        return pltpu.make_async_remote_copy(
            src_ref=part.at[rows],
            dst_ref=in_line.at[r - 1],
            send_sem=send_b.at[r - 1],
            recv_sem=recv_b.at[r - 1],
            device_id=where,
            device_id_type=pl.DeviceIdType.MESH,
        )

    def copy_c(r):
        peer, where = line_peer(r)
        return pltpu.make_async_remote_copy(
            src_ref=line_rows.at[line],
            dst_ref=line_rows.at[line],
            send_sem=send_c.at[r - 1],
            recv_sem=recv_c.at[r - 1],
            device_id=where,
            device_id_type=pl.DeviceIdType.MESH,
        )

    def copy_d(r):
        peer, where = plane_peer(r)
        return pltpu.make_async_remote_copy(
            src_ref=line_rows,
            dst_ref=plane_rows.at[member],
            send_sem=send_d.at[r - 1],
            recv_sem=recv_d.at[r - 1],
            device_id=where,
            device_id_type=pl.DeviceIdType.MESH,
        )

    def each(count, action):
        def one(r, carry):
            action(r)
            return carry

        lax.fori_loop(1, count, one, 0)

    @pl.when(step == 0)
    def _():
        barrier = pltpu.get_barrier_semaphore()

        def greet(where):
            pl.semaphore_signal(
                barrier, inc=1, device_id=where, device_id_type=pl.DeviceIdType.MESH
            )

        each(members, lambda r: greet(plane_peer(r)[1]))
        each(lines, lambda r: greet(line_peer(r)[1]))
        pl.semaphore_wait(barrier, members + lines - 2)
        each(members, lambda r: copy_a(r).start())

        blocks = left_ref.shape[0]
        for at, strip in enumerate((left_ref, mid_ref, right_ref)):

            def spread(n, carry):
                rows = strip[pl.ds(pl.multiple_of(n * 16, 16), 16), :].astype(jnp.float32)
                pool[pl.ds(at * blocks + n * 16, 16)] = jnp.broadcast_to(
                    rows[:, None, :], (16, 8, channels)
                )
                return carry

            lax.fori_loop(0, blocks // 16, spread, 0)

    @pl.when(step == 8)
    def _():
        each(members, lambda r: copy_a(r).wait_recv())
        part[...] = sums_ref[pl.ds(pl.multiple_of(member * chunk, 8), chunk), :]

        def add(r):
            part[...] += in_plane[r - 1]

        each(members, add)
        each(lines, lambda r: copy_b(r).start())

    @pl.when(step == 10)
    def _():
        each(lines, lambda r: copy_b(r).wait_recv())
        owned = part[pl.ds(pl.multiple_of(line * share, 8), share), :]
        for r in range(1, lines):
            owned = owned + in_line[r - 1]
        stacked = jnp.concatenate([owned[:, :channels], owned[:, channels:]], axis=0)
        scaled = stacked * norm_factor * filter_ref[...]
        line_rows[line] = jnp.dot(
            scaled,
            w_mix[...],
            precision=lax.Precision.HIGHEST,
            preferred_element_type=jnp.float32,
        ).astype(jnp.bfloat16)
        each(lines, lambda r: copy_c(r).start())

    @pl.when(step == 12)
    def _():
        each(lines, lambda r: copy_c(r).wait_recv())
        each(members, lambda r: copy_d(r).start())

    recv[...] = jnp.dot(feat_ref[...], w_recv[...], preferred_element_type=jnp.float32)
    atoms = feat_ref.shape[0]

    def some_atoms(it, carry):
        edge_rows(degree, 8, it, snd_ref, pool, basis_ref, w_basis, recv, total)
        return carry

    lax.fori_loop(0, atoms // 8, some_atoms, 0)
    high = total[...].astype(jnp.bfloat16)
    low_part = (total[...] - high.astype(jnp.float32)).astype(jnp.bfloat16)
    agg_ref[...] = (
        jnp.dot(high, w_out[...], preferred_element_type=jnp.float32)
        + jnp.dot(low_part, w_out[...], preferred_element_type=jnp.float32)
    ) * (1.0 / math.sqrt(degree))

    @pl.when(step == pl.num_programs(0) - 1)
    def _():
        each(members, lambda r: copy_a(r).wait_send())
        each(lines, lambda r: copy_b(r).wait_send())
        each(lines, lambda r: copy_c(r).wait_send())
        each(members, lambda r: copy_d(r).wait())
        plane_rows[member] = line_rows[...]
        grid_rows = factor_ref.shape[0] // 2

        def lay(n, carry):
            rows = plane_rows[n // lines, n % lines].astype(jnp.float32)
            factor_ref[pl.ds(pl.multiple_of(n * share, 8), share), :] = rows[:share]
            factor_ref[pl.ds(pl.multiple_of(grid_rows + n * share, 8), share), :] = rows[share:]
            return carry

        lax.fori_loop(0, members * lines, lay, 0)


def finish_kernel(scale, table_ref, factors_ref, agg_ref, mask_ref, out_ref):
    spread = lax.dot_general(
        factors_ref[...].astype(jnp.bfloat16), table_ref[...], CONTRACT_FIRST, preferred_element_type=jnp.float32
    )
    out_ref[...] = mask_ref[...] * (agg_ref[...] + spread.T * scale)


def whole(shape):
    return pl.BlockSpec(shape, lambda i: (0,) * len(shape), pipeline_mode=pl.Buffered(1))


def edges_and_factors(
    features, strips, senders, edge_basis, w_recv, w_basis, w_out, sums, filter_rows, w_mix, plan
):
    degree, cols, low, members, lines, share, norm_factor = plan
    atom_rows, channels = features.shape
    grid_rows = sums.shape[0]
    step = 64
    pool_rows = sum(strip.shape[0] for strip in strips)
    dma = pltpu.SemaphoreType.DMA
    return pl.pallas_call(
        lambda *refs: fused_kernel(plan, *refs),
        grid=(atom_rows // step,),
        in_specs=[
            pl.BlockSpec((step * degree,), lambda i: (i,), memory_space=pltpu.SMEM),
            *[whole(strip.shape) for strip in strips],
            pl.BlockSpec((edge_basis.shape[0], step * degree), lambda i: (0, i)),
            pl.BlockSpec((step, channels), lambda i: (i, 0)),
            whole(w_recv.shape),
            whole(w_basis.shape),
            whole(w_out.shape),
            whole(sums.shape),
            whole(filter_rows.shape),
            whole(w_mix.shape),
        ],
        out_specs=[
            pl.BlockSpec((step, channels), lambda i: (i, 0)),
            whole((2 * grid_rows, channels)),
        ],
        out_shape=[
            jax.ShapeDtypeStruct((atom_rows, channels), jnp.float32),
            jax.ShapeDtypeStruct((2 * grid_rows, channels), jnp.float32),
        ],
        scratch_shapes=[
            pltpu.VMEM((pool_rows, 8, channels), jnp.float32),
            pltpu.VMEM((step, channels), jnp.float32),
            pltpu.VMEM((step, channels), jnp.float32),
            pltpu.VMEM((members - 1, lines * share, 2 * channels), jnp.float32),
            pltpu.VMEM((lines * share, 2 * channels), jnp.float32),
            pltpu.VMEM((lines - 1, share, 2 * channels), jnp.float32),
            pltpu.VMEM((lines, 2 * share, channels), jnp.bfloat16),
            pltpu.VMEM((members, lines, 2 * share, channels), jnp.bfloat16),
            dma((members - 1,)),
            dma((members - 1,)),
            dma((lines - 1,)),
            dma((lines - 1,)),
            dma((lines - 1,)),
            dma((lines - 1,)),
            dma((members - 1,)),
            dma((members - 1,)),
        ],
        compiler_params=pltpu.CompilerParams(
            vmem_limit_bytes=56 * MIB, collective_id=0, has_side_effects=True
        ),
        cost_estimate=pl.CostEstimate(
            flops=atom_rows * degree * channels * 200,
            bytes_accessed=atom_rows * degree * channels * 16,
            transcendentals=atom_rows * degree * channels,
        ),
        name="edges",
    )(
        senders, *strips, edge_basis, features, w_recv, w_basis, w_out, sums, filter_rows, w_mix
    )


def shifted(cells, axis, by):
    count = lax.axis_size(axis)
    return lax.ppermute(cells, axis, [(i, (i + by) % count) for i in range(count)])


def per_device(
    features,
    positions,
    atom_count,
    kgrid,
    k_filter,
    w_mix,
    w_recv,
    w_send,
    w_basis,
    w_out,
    edge_basis,
    senders,
):
    atom_rows, channels = features.shape
    degree = senders.shape[0] // atom_rows
    total_k = kgrid.shape[1]
    devices = lax.axis_size(("slab", "sub"))
    cols = lax.axis_size("sub")
    unit = devices * 8
    grid_rows = -(-SIDE * PAIRS // unit) * unit
    share = grid_rows // devices
    norm_factor = 1.0 / math.sqrt(atom_rows * devices)
    live_mask = (jnp.arange(atom_rows, dtype=jnp.int32) < atom_count[0]).astype(jnp.float32)
    masked = (features.astype(jnp.float32) * live_mask[:, None]).astype(jnp.bfloat16)

    send_proj = jnp.dot(features, w_send, preferred_element_type=jnp.float32).astype(jnp.bfloat16)
    if cols == 2:
        strip = jnp.stack([send_proj, shifted(send_proj, "sub", 1)])
    else:
        strip = jnp.stack([shifted(send_proj, "sub", 1), send_proj, shifted(send_proj, "sub", -1)])
    strip = strip.reshape(-1, channels)
    strips = (shifted(strip, "slab", 1), strip, shifted(strip, "slab", -1))
    if cols == 2:
        block = senders // atom_rows
        slab_step = block // 3
        col_step = block - 3 * slab_step
        senders = (slab_step * 2 + (col_step != 1)) * atom_rows + (senders - block * atom_rows)

    steps = jnp.arange(16, dtype=jnp.float32)
    waves = jnp.concatenate([steps, steps - KMAX, steps - KMAX])
    turns = waves[:, None] * jnp.repeat(positions, 16, axis=0)
    angles = (turns - jnp.round(turns)) * (2.0 * math.pi)
    table, sums = pl.pallas_call(
        table_kernel,
        out_shape=[
            jax.ShapeDtypeStruct((2 * grid_rows, atom_rows), jnp.bfloat16),
            jax.ShapeDtypeStruct((grid_rows, 2 * channels), jnp.float32),
        ],
        scratch_shapes=[pltpu.VMEM((PAIRS, atom_rows), jnp.float32)] * 2,
        compiler_params=pltpu.CompilerParams(vmem_limit_bytes=32 * MIB),
        name="factors",
    )(jnp.cos(angles), jnp.sin(angles), masked)

    low = 4
    lines = lax.axis_size("slab") // low
    members = low * cols
    slab, sub = lax.axis_index("slab"), lax.axis_index("sub")
    piece = ((slab % low) * cols + sub) * lines + slab // low
    flip = jnp.where(kgrid[0] < 0, -1, 1)
    grid_of_k = (kgrid[2] * flip + KMAX) * PAIRS + kgrid[0] * flip * SIDE + kgrid[1] * flip + KMAX
    my_rows = piece * share + jnp.arange(share, dtype=jnp.int32)
    picks = (my_rows[:, None] == grid_of_k[None, :]).astype(jnp.float32)
    filter_sum = jnp.dot(
        picks, k_filter, precision=lax.Precision.HIGHEST, preferred_element_type=jnp.float32
    )
    filter_rows = jnp.concatenate([filter_sum, filter_sum])
    plan = (degree, cols, low, members, lines, share, norm_factor)
    aggregate, factors = edges_and_factors(
        features, strips, senders, edge_basis, w_recv, w_basis, w_out, sums, filter_rows, w_mix, plan
    )
    return pl.pallas_call(
        lambda *refs: finish_kernel(4.0 / math.sqrt(total_k), *refs),
        out_shape=jax.ShapeDtypeStruct((atom_rows, channels), jnp.float32),
        compiler_params=pltpu.CompilerParams(vmem_limit_bytes=32 * MIB),
        name="finish",
    )(table, factors, aggregate, live_mask[:, None])


def solution(mesh):
    placed = (
        P(("slab", "sub"), None),
        P(None, ("slab", "sub")),
        P(("slab", "sub")),
        P(),
        P(),
        P(),
        P(),
        P(),
        P(),
        P(),
        P(None, ("slab", "sub")),
        P(("slab", "sub")),
    )
    return jax.shard_map(
        per_device, mesh=mesh, in_specs=placed, out_specs=P(("slab", "sub"), None), check_vma=False
    )
```

time: 355 us -> 106 us (0.30)
  the two profiles are of different devices: /device:TPU:0 before, /device:TPU:1 now
where the time goes in v1:
time: 106 us
  Pallas kernels  72.1 us (68%)
  waiting for transfers between devices  13.4 us (13%)
  local copies, waits for them, and re-layouts  9.04 us (9%)
  other arithmetic  4.51 us (4%)
  starting transfers between devices  4.24 us (4%)
  matrix products  1.76 us (2%)
    pallas_call x1, Pallas kernels, edges_and_factors(): pl.pallas_call(lambda *refs: fused_kernel(plan, *refs), grid=(atom_rows /...  66.5 us
    ppermute x3, waiting for transfers between devices, shifted(): lax.ppermute(cells, axis, [(i, (i + by) % count) for i in range(count)])  13.4 us
    unnamed x22, local copies, waits for them, and re-layouts  9.04 us
    ppermute x3, starting transfers between devices, shifted(): lax.ppermute(cells, axis, [(i, (i + by) % count) for i in range(count)])  4.24 us
    pallas_call x1, Pallas kernels, per_device(): pl.pallas_call(table_kernel, out_shape=[jax.ShapeDtypeStruct((2 * grid_ro...  3.78 us
  transfers between devices with their start and end apart: 3, of which 2 were waited for; matrix products, arithmetic and copies ran while one was open for 5% of the time, Pallas kernels for 4%

profile of v1, /device:TPU:1, one launch (start us, length us, event | category | flops | bytes accessed | tf_op | source)
XLA Modules:
  0.0 105.9 jit_solution(10541576248926268436)
XLA Ops:
  0.0 0.0 copy-start
  0.0 0.0 copy-start.8
  0.0 1.2 %convolution_convert_fusion = bf16[1024,128]{1,0:T(8,128)(2,1)S(1)} fusion(bf16[1024,128]{1,0:T(8,128)(2,1)} %refs_5_.1, bf16[128,128]{1,0:T(8,128)(2,1)} %param.19), kind=kOutput, calls=%fused_computation | convolution fusion | flops 33685504 | bytes 557056 | tf_op jit(solution)/shard_map/dot_general | solution.py:381
  1.3 2.1 %collective-permute-start = (bf16[1024,128]{1,0:T(8,128)(2,1)S(1)}, bf16[1024,128]{1,0:T(8,128)(2,1)S(1)}, u32[]{:S(2)}, u32[]{:S(2)}) collective-permute-start(bf16[1024,128]{1,0:T(8,128)(2,1)S(1)} %convolution_convert_fusion), channel_id=1, source_target_pairs={{0,1},{1,0},{2,3},{3,2},{4,5},{5,4},{6,7},{7,6},{8,9},{9,8},{10,11... | collective-permute-start | bytes 786440 | tf_op jit(solution)/shard_map/ppermute | solution.py:352
  4.0 1.2 %multiply_convert_fusion.masked_ref = bf16[1024,128]{1,0:T(8,128)(2,1)S(1)} fusion(bf16[1024,128]{1,0:T(8,128)(2,1)} %refs_5_.1, f32[1024]{0:T(1024)S(1)} %fusion.11), kind=kLoop, calls=%fused_computation.3 | loop fusion | flops 393216 | bytes 528384 | tf_op jit(solution)/shard_map/convert_element_type | solution.py:379
  5.2 0.9 add_add_fusion
  6.1 0.0 copy-done
  6.1 0.5 fusion.1
  6.7 0.1 pad_maximum_fusion.2
  6.8 0.0 copy-done.8
  6.8 0.0 copy-start.7
  6.8 0.8 fusion.4
  7.6 3.8 %factors.1 = (bf16[2560,1024]{1,0:T(8,128)(2,1)S(1)}, f32[1280,256]{1,0:T(8,128)S(1)}) custom-call(f32[48,1024]{1,0:T(8,128)S(1)} %get-tuple-element.14.base_cos, f32[48,1024]{1,0:T(8,128)S(1)} %get-tuple-element.13.base_sin, bf16[1024,128]{1,0:T(8,128)(2,1)S(1)} %multiply_convert_fusion.masked_ref), custom_call_target="tpu_custom_call" | custom-call | tf_op jit(solution)/shard_map/factors/pallas_call | solution.py:398
  11.3 0.0 copy-start.1
  11.3 2.3 %copy-done.1 = bf16[2560,1024]{1,0:T(8,128)(2,1)} copy-done((bf16[2560,1024]{1,0:T(8,128)(2,1)}, bf16[2560,1024]{1,0:T(8,128)(2,1)S(1)}, u32[]{:S(2)}) %copy-start.1) | copy-done | bytes 5242904
  13.6 0.0 copy-start.5
  13.6 1.1 %copy-done.5 = f32[1280,256]{1,0:T(8,128)} copy-done((f32[1280,256]{1,0:T(8,128)}, f32[1280,256]{1,0:T(8,128)S(1)}, u32[]{:S(2)}) %copy-start.5) | copy-done | bytes 1310744
  14.7 0.6 pad_maximum_fusion.1.refs_10_
  15.3 0.1 fusion.refs_3_
  15.4 0.0 collective-permute-done
  15.4 0.1 pad_maximum_fusion
  15.5 0.0 copy-start.6
  15.5 2.1 %collective-permute-start.1 = (bf16[2048,128]{1,0:T(8,128)(2,1)S(1)}, bf16[2048,128]{1,0:T(8,128)(2,1)S(1)}, u32[]{:S(2)}, u32[]{:S(2)}) collective-permute-start(bf16[2048,128]{1,0:T(8,128)(2,1)S(1)} %bitcast.19), channel_id=1, source_target_pairs={{0,2},{2,4},{4,6},{6,8},{8,10},{10,12},{12,14},{14,16},{16,18},{18... | collective-permute-start | bytes 1572872 | tf_op jit(solution)/shard_map/ppermute | solution.py:352
  17.6 0.0 collective-permute-start.2
  17.6 0.0 copy-done.7
  17.6 0.9 subtract_add_fusion.refs_0_
  18.5 10.9 %collective-permute-done.1.refs_1_ = bf16[2048,128]{1,0:T(8,128)(2,1)S(1)} collective-permute-done((bf16[2048,128]{1,0:T(8,128)(2,1)S(1)}, bf16[2048,128]{1,0:T(8,128)(2,1)S(1)}, u32[]{:S(2)}, u32[]{:S(2)}) %collective-permute-start.1) | collective-permute-done | bytes 524320 | tf_op jit(solution)/shard_map/ppermute | solution.py:352
  29.3 0.0 copy-start.9
  29.3 2.5 %collective-permute-done.2.refs_3_ = bf16[2048,128]{1,0:T(8,128)(2,1)S(1)} collective-permute-done((bf16[2048,128]{1,0:T(8,128)(2,1)S(1)}, bf16[2048,128]{1,0:T(8,128)(2,1)S(1)}, u32[]{:S(2)}, u32[]{:S(2)}) %collective-permute-start.2) | collective-permute-done | bytes 524320 | tf_op jit(solution)/shard_map/ppermute | solution.py:352
  31.8 0.0 copy-start.10
  31.8 0.0 copy-done.6
  31.8 0.0 copy-done.9
  31.8 0.8 copy-done.10
  32.6 66.5 %edges.1 = (f32[1024,128]{1,0:T(8,128)}, f32[2560,128]{1,0:T(8,128)}) custom-call(s32[32768]{0:T(1024)} %subtract_add_fusion.refs_0_, bf16[2048,128]{1,0:T(8,128)(2,1)} %copy-done.9, bf16[2048,128]{1,0:T(8,128)(2,1)} %bitcast.21, bf16[2048,128]{1,0:T(8,128)(2,1)} %copy-done.10, bf16[8,32768]{1,0:T(8,128)(2,1)} %refs_4_.1, bf16[1024,128]{1,0:T(8,128)(2,1)} %refs_5_.1, ...), custom_call_target="tpu_custom_call" | custom-call | flops 838860800 | bytes 67108864 | tf_op jit(solution)/shard_map/edges/pallas_call | solution.py:295
  99.2 0.0 copy-start.2
  99.2 2.5 %copy-done.2 = bf16[2560,1024]{1,0:T(8,128)(2,1)S(1)} copy-done((bf16[2560,1024]{1,0:T(8,128)(2,1)S(1)}, bf16[2560,1024]{1,0:T(8,128)(2,1)}, u32[]{:S(2)}) %copy-start.2) | copy-done | bytes 5242904
  101.7 0.0 copy-start.3
  101.7 1.3 %copy-done.3 = f32[2560,128]{1,0:T(8,128)S(1)} copy-done((f32[2560,128]{1,0:T(8,128)S(1)}, f32[2560,128]{1,0:T(8,128)}, u32[]{:S(2)}) %copy-start.3) | copy-done | bytes 1310744
  103.0 0.0 copy-start.4
  103.0 1.0 copy-done.4
  104.0 1.8 %finish.1 = f32[1024,128]{1,0:T(8,128)} custom-call(bf16[2560,1024]{1,0:T(8,128)(2,1)S(1)} %copy-done.2, f32[2560,128]{1,0:T(8,128)S(1)} %copy-done.3, f32[1024,128]{1,0:T(8,128)S(1)} %copy-done.4, f32[1024,1]{1,0:T(8,128)S(1)} %fusion.refs_3_), custom_call_target="tpu_custom_call" | custom-call | tf_op jit(solution)/shard_map/finish/pallas_call | solution.py:426
  (4 shorter events, 0.0 us)
Async XLA Ops:
  0.0 6.1 %copy-start = (f32[2048,128]{1,0:T(8,128)S(1)}, f32[2048,128]{1,0:T(8,128)}, u32[]{:S(2)}) copy-start(f32[2048,128]{1,0:T(8,128)} %param.16) | copy-start | bytes 3145732
  0.0 6.8 %copy-start.8 = (f32[3,1024]{1,0:T(4,128)S(1)}, f32[3,1024]{1,0:T(4,128)}, u32[]{:S(2)}) copy-start(f32[3,1024]{1,0:T(4,128)} %param.13) | copy-start | bytes 36868
  1.3 14.1 %collective-permute-start = (bf16[1024,128]{1,0:T(8,128)(2,1)S(1)}, bf16[1024,128]{1,0:T(8,128)(2,1)S(1)}, u32[]{:S(2)}, u32[]{:S(2)}) collective-permute-start(bf16[1024,128]{1,0:T(8,128)(2,1)S(1)} %convolution_convert_fusion), channel_id=1, source_target_pairs={{0,1},{1,0},{2,3},{3,2},{4,5},{5,4},{6,7},{7,6},{8,9},{9,8},{10,11... | collective-permute-start | bytes 786440 | tf_op jit(solution)/shard_map/ppermute | solution.py:352
  6.8 10.8 %copy-start.7 = (s32[32768]{0:T(1024)S(1)}, s32[32768]{0:T(1024)}, u32[]{:S(2)}) copy-start(s32[32768]{0:T(1024)} %param.23) | copy-start | bytes 393220
  11.3 2.3 %copy-start.1 = (bf16[2560,1024]{1,0:T(8,128)(2,1)}, bf16[2560,1024]{1,0:T(8,128)(2,1)S(1)}, u32[]{:S(2)}) copy-start(bf16[2560,1024]{1,0:T(8,128)(2,1)S(1)} %get-tuple-element.9.refs_0_) | copy-start | bytes 15728644
  13.6 1.1 %copy-start.5 = (f32[1280,256]{1,0:T(8,128)}, f32[1280,256]{1,0:T(8,128)S(1)}, u32[]{:S(2)}) copy-start(f32[1280,256]{1,0:T(8,128)S(1)} %get-tuple-element.10.refs_9_) | copy-start | bytes 3932164
  15.5 16.4 %copy-start.6 = (bf16[2,1024,128]{2,1,0:T(8,128)(2,1)}, bf16[2,1024,128]{2,1,0:T(8,128)(2,1)S(1)}, u32[]{:S(2)}) copy-start(bf16[2,1024,128]{2,1,0:T(8,128)(2,1)S(1)} %pad_maximum_fusion) | copy-start | bytes 1572868
  15.5 13.9 %collective-permute-start.1 = (bf16[2048,128]{1,0:T(8,128)(2,1)S(1)}, bf16[2048,128]{1,0:T(8,128)(2,1)S(1)}, u32[]{:S(2)}, u32[]{:S(2)}) collective-permute-start(bf16[2048,128]{1,0:T(8,128)(2,1)S(1)} %bitcast.19), channel_id=1, source_target_pairs={{0,2},{2,4},{4,6},{6,8},{8,10},{10,12},{12,14},{14,16},{16,18},{18... | collective-permute-start | bytes 1572872 | tf_op jit(solution)/shard_map/ppermute | solution.py:352
  17.6 14.2 %collective-permute-start.2 = (bf16[2048,128]{1,0:T(8,128)(2,1)S(1)}, bf16[2048,128]{1,0:T(8,128)(2,1)S(1)}, u32[]{:S(2)}, u32[]{:S(2)}) collective-permute-start(bf16[2048,128]{1,0:T(8,128)(2,1)S(1)} %bitcast.20), channel_id=1, source_target_pairs={{0,30},{2,0},{4,2},{6,4},{8,6},{10,8},{12,10},{14,12},{16,14},{18,... | collective-permute-start | bytes 1572872 | tf_op jit(solution)/shard_map/ppermute | solution.py:352
  29.3 2.5 %copy-start.9 = (bf16[2048,128]{1,0:T(8,128)(2,1)}, bf16[2048,128]{1,0:T(8,128)(2,1)S(1)}, u32[]{:S(2)}) copy-start(bf16[2048,128]{1,0:T(8,128)(2,1)S(1)} %collective-permute-done.1.refs_1_) | copy-start | bytes 1572868
  31.8 0.8 copy-start.10
  99.2 2.5 %copy-start.2 = (bf16[2560,1024]{1,0:T(8,128)(2,1)S(1)}, bf16[2560,1024]{1,0:T(8,128)(2,1)}, u32[]{:S(2)}) copy-start(bf16[2560,1024]{1,0:T(8,128)(2,1)} %copy-done.1) | copy-start | bytes 15728644
  101.7 1.3 %copy-start.3 = (f32[2560,128]{1,0:T(8,128)S(1)}, f32[2560,128]{1,0:T(8,128)}, u32[]{:S(2)}) copy-start(f32[2560,128]{1,0:T(8,128)} %get-tuple-element.11.refs_1_) | copy-start | bytes 3932164
  103.0 1.0 copy-start.4

commit v2 on v1

v2 whole, which is shorter than its diff:
```python
import math

import jax
import jax.numpy as jnp
from jax import lax
from jax.experimental import pallas as pl
from jax.experimental.pallas import tpu as pltpu
from jax.sharding import PartitionSpec as P

KMAX = 6
SIDE = 2 * KMAX + 1
PAIRS = 96
MIB = 1024 * 1024
CONTRACT_FIRST = (((0,), (0,)), ((), ()))


def fill_tables(base_cos, base_sin, masked_ref, table_ref, sums_ref, pair_cos, pair_sin):
    grid_rows = table_ref.shape[0] // 2
    channels = masked_ref.shape[1]
    atom_rows = masked_ref.shape[0]
    for a in range(KMAX + 1):
        cx, sx = base_cos[a : a + 1, :], base_sin[a : a + 1, :]
        cy, sy = base_cos[16 : 16 + SIDE, :], base_sin[16 : 16 + SIDE, :]
        pair_cos[a * SIDE : (a + 1) * SIDE, :] = cx * cy - sx * sy
        pair_sin[a * SIDE : (a + 1) * SIDE, :] = sx * cy + cx * sy
    used = (KMAX + 1) * SIDE
    pair_cos[used:, :] = jnp.zeros((PAIRS - used, atom_rows), jnp.float32)
    pair_sin[used:, :] = jnp.zeros((PAIRS - used, atom_rows), jnp.float32)

    def one_plane(q, carry):
        cz, sz = base_cos[pl.ds(32 + q, 1), :], base_sin[pl.ds(32 + q, 1), :]
        cosines = (pair_cos[...] * cz - pair_sin[...] * sz).astype(jnp.bfloat16)
        sines = (pair_sin[...] * cz + pair_cos[...] * sz).astype(jnp.bfloat16)
        at = pl.multiple_of(q * PAIRS, PAIRS)
        table_ref[pl.ds(at, PAIRS), :] = cosines
        table_ref[pl.ds(at + grid_rows, PAIRS), :] = sines
        sums_ref[pl.ds(at, PAIRS), :channels] = jnp.dot(
            cosines, masked_ref[...], preferred_element_type=jnp.float32
        ).astype(jnp.bfloat16).astype(jnp.bfloat16)
        sums_ref[pl.ds(at, PAIRS), channels:] = jnp.dot(
            sines, masked_ref[...], preferred_element_type=jnp.float32
        ).astype(jnp.bfloat16)
        return carry

    lax.fori_loop(0, SIDE, one_plane, 0)
    tail = grid_rows - SIDE * PAIRS
    if tail:
        for start in (SIDE * PAIRS, grid_rows + SIDE * PAIRS):
            table_ref[start : start + tail, :] = jnp.zeros((tail, atom_rows), jnp.bfloat16)
        sums_ref[SIDE * PAIRS :, :] = jnp.zeros((tail, 2 * channels), jnp.bfloat16)


def edge_rows(degree, group, it, snd_ref, pool, basis_ref, w_basis, recv, total):
    edges = group * degree
    first = pl.multiple_of(it * edges, edges)
    row = pl.multiple_of(it * group, group)
    sublane = lax.broadcasted_iota(jnp.int32, pool.shape[1:], 0)
    recv_rows = recv[pl.ds(row, group), :]
    together = 128 // degree
    sums = []
    for j in range(group):
        if j % together == 0:
            radial = lax.dot_general(
                basis_ref[:, pl.ds(pl.multiple_of(first + j * degree, 128), 128)],
                w_basis[...],
                CONTRACT_FIRST,
                preferred_element_type=jnp.float32,
            )
        octets = []
        for octet in range(degree // 8):
            start = first + j * degree + octet * 8
            picked = pool[snd_ref[start]]
            for k in range(1, 8):
                picked = jnp.where(sublane == k, pool[snd_ref[start + k]], picked)
            octets.append(picked)
        gathered = jnp.concatenate(octets, axis=0)
        at = j % together * degree
        v = gathered + radial[at : at + degree, :] + recv_rows[j : j + 1, :]
        half = 0.5 * v
        hidden = (half + half * jnp.tanh(half)).astype(jnp.bfloat16)
        sums.append(jnp.sum(hidden.astype(jnp.float32), axis=0, keepdims=True))
    total[pl.ds(row, group), :] = jnp.concatenate(sums, axis=0)


def fused_kernel(
    plan,
    snd_ref,
    basis_ref,
    feat_ref,
    count_ref,
    base_cos,
    base_sin,
    w_send,
    w_recv,
    w_basis,
    w_out,
    filter_ref,
    w_mix,
    out_ref,
    strips,
    pool,
    masked,
    pair_cos,
    pair_sin,
    table,
    sums_ref,
    factor_ref,
    recv,
    total,
    in_plane,
    part,
    in_line,
    line_rows,
    plane_rows,
    send_a,
    recv_a,
    send_b,
    recv_b,
    send_c,
    recv_c,
    send_d,
    recv_d,
    send_x,
    recv_x,
    send_z,
    recv_z,
):
    degree, cols, low, members, lines, share, norm_factor, scale = plan
    block_rows, channels = feat_ref.shape
    slabs = low * lines
    home = 0 if cols == 2 else 1
    blocks = strips.shape[1]
    step = pl.program_id(0)
    slab, sub = lax.axis_index("slab"), lax.axis_index("sub")
    line = slab // low
    member = (slab % low) * cols + sub
    chunk = lines * share

    def plane_peer(r):
        peer = (member + r) % members
        return peer, {"slab": line * low + peer // cols, "sub": peer % cols}

    def line_peer(r):
        peer = (line + r) % lines
        return peer, {"slab": peer * low + slab % low, "sub": sub}

    def copy_a(r):
        peer, where = plane_peer(r)
        rows = pl.ds(pl.multiple_of(peer * chunk, 16), chunk)
        return pltpu.make_async_remote_copy(
            src_ref=sums_ref.at[rows],
            dst_ref=in_plane.at[r - 1],
            send_sem=send_a.at[r - 1],
            recv_sem=recv_a.at[r - 1],
            device_id=where,
            device_id_type=pl.DeviceIdType.MESH,
        )

    def copy_b(r):
        peer, where = line_peer(r)
        rows = pl.ds(pl.multiple_of(peer * share, 8), share)
        return pltpu.make_async_remote_copy(
            src_ref=part.at[rows],
            dst_ref=in_line.at[r - 1],
            send_sem=send_b.at[r - 1],
            recv_sem=recv_b.at[r - 1],
            device_id=where,
            device_id_type=pl.DeviceIdType.MESH,
        )

    def copy_c(r):
        peer, where = line_peer(r)
        return pltpu.make_async_remote_copy(
            src_ref=line_rows.at[line],
            dst_ref=line_rows.at[line],
            send_sem=send_c.at[r - 1],
            recv_sem=recv_c.at[r - 1],
            device_id=where,
            device_id_type=pl.DeviceIdType.MESH,
        )

    def copy_d(r):
        peer, where = plane_peer(r)
        return pltpu.make_async_remote_copy(
            src_ref=line_rows,
            dst_ref=plane_rows.at[member],
            send_sem=send_d.at[r - 1],
            recv_sem=recv_d.at[r - 1],
            device_id=where,
            device_id_type=pl.DeviceIdType.MESH,
        )

    def each(count, action):
        def one(r, carry):
            action(r)
            return carry

        lax.fori_loop(1, count, one, 0)

    sides = [(1, 1)] if cols == 2 else [(1, 0), (-1, 2)]

    def column_of(by):
        return {"slab": slab, "sub": (sub + by + cols) % cols}

    def slab_of(by):
        return {"slab": (slab + by + slabs) % slabs, "sub": sub}

    def copy_x(n):
        by, slot = sides[n]
        return pltpu.make_async_remote_copy(
            src_ref=strips.at[1, home],
            dst_ref=strips.at[1, slot],
            send_sem=send_x.at[n],
            recv_sem=recv_x.at[n],
            device_id=column_of(by),
            device_id_type=pl.DeviceIdType.MESH,
        )

    def copy_z(up, c):
        return pltpu.make_async_remote_copy(
            src_ref=strips.at[1, c],
            dst_ref=strips.at[0 if up else 2, c],
            send_sem=send_z.at[up * blocks + c],
            recv_sem=recv_z.at[up * blocks + c],
            device_id=slab_of(1 if up else -1),
            device_id_type=pl.DeviceIdType.MESH,
        )

    def spread(a, c):
        base = (a * blocks + c) * block_rows

        def some(n, carry):
            at = pl.multiple_of(n * 16, 16)
            rows = strips[a, c, pl.ds(at, 16), :].astype(jnp.float32)
            pool[pl.ds(base + at, 16)] = jnp.broadcast_to(rows[:, None, :], (16, 8, channels))
            return carry

        lax.fori_loop(0, block_rows // 16, some, 0)

    def live(width):
        rows = lax.broadcasted_iota(jnp.int32, (block_rows, width), 0)
        return rows < count_ref[0]

    @pl.when(step == 0)
    def _():
        strips[1, home] = jnp.dot(
            feat_ref[...], w_send[...], preferred_element_type=jnp.float32
        ).astype(jnp.bfloat16)
        barrier = pltpu.get_barrier_semaphore()

        def greet(where):
            pl.semaphore_signal(
                barrier, inc=1, device_id=where, device_id_type=pl.DeviceIdType.MESH
            )

        each(members, lambda r: greet(plane_peer(r)[1]))
        each(lines, lambda r: greet(line_peer(r)[1]))
        for by, slot in sides:
            greet(column_of(by))
        greet(slab_of(1))
        greet(slab_of(-1))
        pl.semaphore_wait(barrier, members + lines + len(sides))
        for n in range(len(sides)):
            copy_x(n).start()
        for up in (1, 0):
            copy_z(up, home).start()
        masked[...] = jnp.where(live(channels), feat_ref[...].astype(jnp.float32), 0.0).astype(
            jnp.bfloat16
        )
        fill_tables(base_cos, base_sin, masked, table, sums_ref, pair_cos, pair_sin)
        for n, (by, slot) in enumerate(sides):
            copy_x(n).wait_recv()
            for up in (1, 0):
                copy_z(up, slot).start()
        each(members, lambda r: copy_a(r).start())
        recv[...] = jnp.dot(feat_ref[...], w_recv[...], preferred_element_type=jnp.float32)
        for c in range(blocks):
            spread(1, c)
        for c in [home] + [slot for by, slot in sides]:
            for up in (1, 0):
                copy_z(up, c).wait_recv()
                spread(0 if up else 2, c)

    @pl.when(step == 3)
    def _():
        each(members, lambda r: copy_a(r).wait_recv())
        part[...] = sums_ref[pl.ds(pl.multiple_of(member * chunk, 16), chunk), :].astype(jnp.float32)

        def add(r):
            part[...] += in_plane[r - 1].astype(jnp.float32)

        each(members, add)
        each(lines, lambda r: copy_b(r).start())

    @pl.when(step == 6)
    def _():
        each(lines, lambda r: copy_b(r).wait_recv())
        owned = part[pl.ds(pl.multiple_of(line * share, 8), share), :]
        for r in range(1, lines):
            owned = owned + in_line[r - 1]
        stacked = jnp.concatenate([owned[:, :channels], owned[:, channels:]], axis=0)
        scaled = stacked * norm_factor * filter_ref[...]
        line_rows[line] = jnp.dot(
            scaled,
            w_mix[...],
            precision=lax.Precision.HIGHEST,
            preferred_element_type=jnp.float32,
        ).astype(jnp.bfloat16)
        each(lines, lambda r: copy_c(r).start())

    @pl.when(step == 9)
    def _():
        each(lines, lambda r: copy_c(r).wait_recv())
        each(members, lambda r: copy_d(r).start())

    atoms = snd_ref.shape[0] // degree
    group = 16

    def some_atoms(it, carry):
        edge_rows(degree, group, it, snd_ref, pool, basis_ref, w_basis, recv_now, total_now)
        return carry

    here = pl.ds(pl.multiple_of(step * atoms, atoms), atoms)
    recv_now, total_now = recv.at[here], total.at[here]
    lax.fori_loop(0, atoms // group, some_atoms, 0)

    @pl.when(step == pl.num_programs(0) - 1)
    def _():
        for n in range(len(sides)):
            copy_x(n).wait_send()
        for up in (1, 0):
            for c in range(blocks):
                copy_z(up, c).wait_send()
        each(members, lambda r: copy_a(r).wait_send())
        each(lines, lambda r: copy_b(r).wait_send())
        each(lines, lambda r: copy_c(r).wait_send())
        each(members, lambda r: copy_d(r).wait())
        plane_rows[member] = line_rows[...]
        grid_rows = factor_ref.shape[0] // 2

        def lay(n, carry):
            rows = plane_rows[n // lines, n % lines].astype(jnp.float32)
            factor_ref[pl.ds(pl.multiple_of(n * share, 8), share), :] = rows[:share]
            factor_ref[pl.ds(pl.multiple_of(grid_rows + n * share, 8), share), :] = rows[share:]
            return carry

        lax.fori_loop(0, members * lines, lay, 0)
        spread_t = lax.dot_general(
            factor_ref[...].astype(jnp.bfloat16),
            table[...],
            CONTRACT_FIRST,
            preferred_element_type=jnp.float32,
        )
        high = total[...].astype(jnp.bfloat16)
        low_part = (total[...] - high.astype(jnp.float32)).astype(jnp.bfloat16)
        aggregate = (
            jnp.dot(high, w_out[...], preferred_element_type=jnp.float32)
            + jnp.dot(low_part, w_out[...], preferred_element_type=jnp.float32)
        ) * (1.0 / math.sqrt(degree))
        out_ref[...] = jnp.where(live(channels), aggregate + spread_t.T * scale, 0.0)


def whole(shape):
    return pl.BlockSpec(shape, lambda i: (0,) * len(shape), pipeline_mode=pl.Buffered(1))


def force_step(
    features, atom_count, senders, edge_basis, base_cos, base_sin, weights, filter_rows, w_mix, plan
):
    degree, cols, low, members, lines, share, norm_factor, scale = plan
    atom_rows, channels = features.shape
    grid_rows = members * lines * share
    blocks = 2 if cols == 2 else 3
    step = 64
    dma = pltpu.SemaphoreType.DMA
    f32, bf16 = jnp.float32, jnp.bfloat16
    return pl.pallas_call(
        lambda *refs: fused_kernel(plan, *refs),
        grid=(atom_rows // step,),
        in_specs=[
            pl.BlockSpec((step * degree,), lambda i: (i,), memory_space=pltpu.SMEM),
            pl.BlockSpec((edge_basis.shape[0], step * degree), lambda i: (0, i)),
            whole(features.shape),
            pl.BlockSpec(memory_space=pltpu.SMEM),
            whole(base_cos.shape),
            whole(base_sin.shape),
            *[whole(weight.shape) for weight in weights],
            whole(filter_rows.shape),
            whole(w_mix.shape),
        ],
        out_specs=whole((atom_rows, channels)),
        out_shape=jax.ShapeDtypeStruct((atom_rows, channels), f32),
        scratch_shapes=[
            pltpu.VMEM((3, blocks, atom_rows, channels), bf16),
            pltpu.VMEM((3 * blocks * atom_rows, 8, channels), f32),
            pltpu.VMEM((atom_rows, channels), bf16),
            pltpu.VMEM((PAIRS, atom_rows), f32),
            pltpu.VMEM((PAIRS, atom_rows), f32),
            pltpu.VMEM((2 * grid_rows, atom_rows), bf16),
            pltpu.VMEM((grid_rows, 2 * channels), bf16),
            pltpu.VMEM((2 * grid_rows, channels), f32),
            pltpu.VMEM((atom_rows, channels), f32),
            pltpu.VMEM((atom_rows, channels), f32),
            pltpu.VMEM((members - 1, lines * share, 2 * channels), bf16),
            pltpu.VMEM((lines * share, 2 * channels), f32),
            pltpu.VMEM((lines - 1, share, 2 * channels), f32),
            pltpu.VMEM((lines, 2 * share, channels), bf16),
            pltpu.VMEM((members, lines, 2 * share, channels), bf16),
            *[dma((members - 1,))] * 2,
            *[dma((lines - 1,))] * 4,
            *[dma((members - 1,))] * 2,
            *[dma((blocks - 1,))] * 2,
            *[dma((2 * blocks,))] * 2,
        ],
        compiler_params=pltpu.CompilerParams(
            vmem_limit_bytes=62 * MIB, collective_id=0, has_side_effects=True
        ),
        cost_estimate=pl.CostEstimate(
            flops=atom_rows * degree * channels * 200,
            bytes_accessed=atom_rows * degree * channels * 16,
            transcendentals=atom_rows * degree * channels,
        ),
        name="force_step",
    )(
        senders, edge_basis, features, atom_count, base_cos, base_sin, *weights, filter_rows, w_mix
    )


def per_device(
    features,
    positions,
    atom_count,
    kgrid,
    k_filter,
    w_mix,
    w_recv,
    w_send,
    w_basis,
    w_out,
    edge_basis,
    senders,
):
    atom_rows, channels = features.shape
    degree = senders.shape[0] // atom_rows
    total_k = kgrid.shape[1]
    devices = lax.axis_size(("slab", "sub"))
    cols = lax.axis_size("sub")
    unit = devices * 8
    grid_rows = -(-SIDE * PAIRS // unit) * unit
    share = grid_rows // devices
    norm_factor = 1.0 / math.sqrt(atom_rows * devices)
    if cols == 2:
        block = senders // atom_rows
        slab_step = block // 3
        col_step = block - 3 * slab_step
        senders = (slab_step * 2 + (col_step != 1)) * atom_rows + (senders - block * atom_rows)

    steps = jnp.arange(16, dtype=jnp.float32)
    waves = jnp.concatenate([steps, steps - KMAX, steps - KMAX])
    turns = waves[:, None] * jnp.repeat(positions, 16, axis=0)
    angles = (turns - jnp.round(turns)) * (2.0 * math.pi)
    low = 4
    lines = lax.axis_size("slab") // low
    members = low * cols
    slab, sub = lax.axis_index("slab"), lax.axis_index("sub")
    piece = ((slab % low) * cols + sub) * lines + slab // low
    flip = jnp.where(kgrid[0] < 0, -1, 1)
    grid_of_k = (kgrid[2] * flip + KMAX) * PAIRS + kgrid[0] * flip * SIDE + kgrid[1] * flip + KMAX
    my_rows = piece * share + jnp.arange(share, dtype=jnp.int32)
    picks = (my_rows[:, None] == grid_of_k[None, :]).astype(jnp.float32)
    filter_sum = jnp.dot(
        picks, k_filter, precision=lax.Precision.HIGHEST, preferred_element_type=jnp.float32
    )
    filter_rows = jnp.concatenate([filter_sum, filter_sum])
    plan = (degree, cols, low, members, lines, share, norm_factor, 4.0 / math.sqrt(total_k))
    weights = (w_send, w_recv, w_basis, w_out)
    return force_step(
        features,
        atom_count,
        senders,
        edge_basis,
        jnp.cos(angles),
        jnp.sin(angles),
        weights,
        filter_rows,
        w_mix,
        plan,
    )


def solution(mesh):
    placed = (
        P(("slab", "sub"), None),
        P(None, ("slab", "sub")),
        P(("slab", "sub")),
        P(),
        P(),
        P(),
        P(),
        P(),
        P(),
        P(),
        P(None, ("slab", "sub")),
        P(("slab", "sub")),
    )
    return jax.shard_map(
        per_device, mesh=mesh, in_specs=placed, out_specs=P(("slab", "sub"), None), check_vma=False
    )
```

time: 106 us -> 80.7 us (0.76)
  waiting for transfers between devices: 13.4 us -> 0 us
  local copies, waits for them, and re-layouts: 9.04 us -> 2.23 us
  starting transfers between devices: 4.24 us -> 0 us
  Pallas kernels: 72.1 us -> 73.8 us
  other arithmetic: 4.51 us -> 3.14 us
  matrix products: 1.76 us -> 0.51 us
    ppermute x3 -> x0, waiting for transfers between devices: 13.4 us -> none  [shifted(): lax.ppermute(cells, axis, [(i, (i + by) % count) for i in range(count)])]
    unnamed x22 -> x9, local copies, waits for them, and re-layouts: 9.04 us -> 2.22 us
    ppermute x3 -> x0, starting transfers between devices: 4.24 us -> none  [shifted(): lax.ppermute(cells, axis, [(i, (i + by) % count) for i in range(count)])]
    pallas_call x3 -> x1, Pallas kernels: 72.1 us -> 73.8 us  [force_step(): pl.pallas_call(lambda *refs: fused_kernel(plan, *refs), grid=(atom_rows /...]
    dot_general x1 -> x0, matrix products: 1.25 us -> none  [per_device(): jnp.dot(features, w_send, preferred_element_type=jnp.float32)]
    convert_element_type x3 -> x0, other arithmetic: 1.21 us -> none  [the longest x1 1.15 us: per_device(): (features.astype(jnp.float32) * live_mask[:, None]).astype(jnp.bfloat16)]
  transfers between devices with their start and end apart: 3 -> 0, of which waited for: 2 -> 0; matrix products, arithmetic and copies ran while one was open for 5% -> 0% of each run, Pallas kernels for 4% -> 0%
where the time goes in v2:
time: 80.7 us; the launch traced here: 80.5 us
  Pallas kernels  73.8 us (91%)
  other arithmetic  3.14 us (4%)
  local copies, waits for them, and re-layouts  2.23 us (3%)
    pallas_call x1, Pallas kernels, force_step(): pl.pallas_call(lambda *refs: fused_kernel(plan, *refs), grid=(atom_rows /...  73.8 us
    unnamed x9, local copies, waits for them, and re-layouts  2.22 us

profile of v2, /device:TPU:1, one launch (start us, length us, event | category | flops | bytes accessed | tf_op | source)
XLA Modules:
  0.0 80.5 jit_solution(3144958044007771039)
XLA Ops:
  0.0 0.0 copy-start
  0.0 0.0 copy-start.2
  0.8 0.1 pad_maximum_fusion.1
  0.9 0.0 copy-done.2
  0.9 0.3 copy-done
  1.3 0.0 copy-start.1
  1.3 0.5 fusion
  1.8 0.6 pad_maximum_fusion.refs_10_
  2.4 0.0 copy-done.1
  2.4 0.0 copy-start.3
  2.4 0.9 %subtract_add_fusion.refs_0_ = s32[32768]{0:T(1024)} fusion(s32[32768]{0:T(1024)S(1)} %copy-done.1), kind=kLoop, calls=%fused_computation.15 | loop fusion | flops 1081344 | bytes 262144 | tf_op jit(solution)/shard_map/add | solution.py:456
  3.3 0.0 copy-done.3
  3.3 1.5 %fusion.3 = (f32[48,1024]{1,0:T(8,128)}, f32[48,1024]{1,0:T(8,128)}) fusion(f32[3,1024]{1,0:T(4,128)S(1)} %copy-done.3, f32[48]{0:T(128)S(1)} %pad_maximum_fusion.1), kind=kLoop, calls=%fused_computation.5 | loop fusion | flops 196608 | bytes 405696 | tf_op jit(solution)/shard_map/sin | solution.py:483
  4.8 73.8 %force_step.1 = f32[1024,128]{1,0:T(8,128)} custom-call(s32[32768]{0:T(1024)} %subtract_add_fusion.refs_0_, bf16[8,32768]{1,0:T(8,128)(2,1)} %refs_1_.1, bf16[1024,128]{1,0:T(8,128)(2,1)} %refs_2_.1, s32[1]{0:T(128)S(6)} %copy.14.refs_3_, f32[48,1024]{1,0:T(8,128)} %get-tuple-element.6.refs_4_, f32[48,1024]{1,0:T(8,128)} %get-tuple-element.5.refs_5_, ...), custom_call_target="tpu_custom_call" | custom-call | flops 838860800 | bytes 67108864 | tf_op jit(solution)/shard_map/force_step/pallas_call | solution.py:377
  78.6 1.9 %copy.15 = f32[1024,128]{1,0:T(8,128)} copy(f32[1024,128]{1,0:T(8,128)} %force_step.1) | data formatting | bytes 1048576
  (4 shorter events, 0.1 us)
Async XLA Ops:
  0.0 1.3 %copy-start = (f32[2048,128]{1,0:T(8,128)S(1)}, f32[2048,128]{1,0:T(8,128)}, u32[]{:S(2)}) copy-start(f32[2048,128]{1,0:T(8,128)} %param.16) | copy-start | bytes 3145732
  0.0 0.9 %copy-start.2 = (s32[3,2048]{1,0:T(4,128)S(1)}, s32[3,2048]{1,0:T(4,128)}, u32[]{:S(2)}) copy-start(s32[3,2048]{1,0:T(4,128)} %param.15) | copy-start | bytes 73732
  1.3 1.1 %copy-start.1 = (s32[32768]{0:T(1024)S(1)}, s32[32768]{0:T(1024)}, u32[]{:S(2)}) copy-start(s32[32768]{0:T(1024)} %param.23) | copy-start | bytes 393220
  2.4 0.9 %copy-start.3 = (f32[3,1024]{1,0:T(4,128)S(1)}, f32[3,1024]{1,0:T(4,128)}, u32[]{:S(2)}) copy-start(f32[3,1024]{1,0:T(4,128)} %param.13) | copy-start | bytes 36868

commit v3 on v2

--- a/solution.py
+++ b/solution.py
@@ -50,36 +50,39 @@
         sums_ref[SIDE * PAIRS :, :] = jnp.zeros((tail, 2 * channels), jnp.bfloat16)
 
 
-def edge_rows(degree, group, it, snd_ref, pool, basis_ref, w_basis, recv, total):
+def edge_rows(degree, group, it, snd_ref, pool, base, total):
     edges = group * degree
     first = pl.multiple_of(it * edges, edges)
     row = pl.multiple_of(it * group, group)
-    sublane = lax.broadcasted_iota(jnp.int32, pool.shape[1:], 0)
-    recv_rows = recv[pl.ds(row, group), :]
-    together = 128 // degree
     sums = []
     for j in range(group):
-        if j % together == 0:
-            radial = lax.dot_general(
-                basis_ref[:, pl.ds(pl.multiple_of(first + j * degree, 128), 128)],
-                w_basis[...],
-                CONTRACT_FIRST,
-                preferred_element_type=jnp.float32,
-            )
-        octets = []
-        for octet in range(degree // 8):
-            start = first + j * degree + octet * 8
-            picked = pool[snd_ref[start]]
-            for k in range(1, 8):
-                picked = jnp.where(sublane == k, pool[snd_ref[start + k]], picked)
-            octets.append(picked)
-        gathered = jnp.concatenate(octets, axis=0)
-        at = j % together * degree
-        v = gathered + radial[at : at + degree, :] + recv_rows[j : j + 1, :]
-        half = 0.5 * v
+        at = first + j * degree
+        rows = [pool[pl.ds(snd_ref[at + e], 1), :] for e in range(degree)]
+        half = jnp.concatenate(rows, axis=0) + base[pl.ds(pl.multiple_of(at, degree), degree), :]
         hidden = (half + half * jnp.tanh(half)).astype(jnp.bfloat16)
         sums.append(jnp.sum(hidden.astype(jnp.float32), axis=0, keepdims=True))
     total[pl.ds(row, group), :] = jnp.concatenate(sums, axis=0)
+
+
+def edge_base(degree, basis_ref, w_basis, recv, base):
+    atoms = 8
+    edges = atoms * degree
+    channels = recv.shape[1]
+
+    def some(n, carry):
+        first = pl.multiple_of(n * edges, edges)
+        radial = lax.dot_general(
+            basis_ref[:, pl.ds(first, edges)],
+            w_basis[...],
+            CONTRACT_FIRST,
+            preferred_element_type=jnp.float32,
+        )
+        rows = recv[pl.ds(pl.multiple_of(n * atoms, atoms), atoms), :]
+        both = radial.reshape(atoms, degree, channels) + rows[:, None, :]
+        base[pl.ds(first, edges), :] = 0.5 * both.reshape(edges, channels)
+        return carry
+
+    lax.fori_loop(0, recv.shape[0] // atoms, some, 0)
 
 
 def fused_kernel(
@@ -106,6 +109,7 @@
     sums_ref,
     factor_ref,
     recv,
+    base,
     total,
     in_plane,
     part,
@@ -227,12 +231,12 @@
         )
 
     def spread(a, c):
-        base = (a * blocks + c) * block_rows
+        first = (a * blocks + c) * block_rows
 
         def some(n, carry):
             at = pl.multiple_of(n * 16, 16)
             rows = strips[a, c, pl.ds(at, 16), :].astype(jnp.float32)
-            pool[pl.ds(base + at, 16)] = jnp.broadcast_to(rows[:, None, :], (16, 8, channels))
+            pool[pl.ds(pl.multiple_of(first + at, 16), 16), :] = 0.5 * rows
             return carry
 
         lax.fori_loop(0, block_rows // 16, some, 0)
@@ -274,6 +278,7 @@
                 copy_z(up, slot).start()
         each(members, lambda r: copy_a(r).start())
         recv[...] = jnp.dot(feat_ref[...], w_recv[...], preferred_element_type=jnp.float32)
+        edge_base(degree, basis_ref, w_basis, recv, base)
         for c in range(blocks):
             spread(1, c)
         for c in [home] + [slot for by, slot in sides]:
@@ -317,11 +322,12 @@
     group = 16
 
     def some_atoms(it, carry):
-        edge_rows(degree, group, it, snd_ref, pool, basis_ref, w_basis, recv_now, total_now)
+        edge_rows(degree, group, it, snd_ref, pool, base_now, total_now)
         return carry
 
     here = pl.ds(pl.multiple_of(step * atoms, atoms), atoms)
-    recv_now, total_now = recv.at[here], total.at[here]
+    total_now = total.at[here]
+    base_now = base.at[pl.ds(pl.multiple_of(step * atoms * degree, atoms * degree), atoms * degree)]
     lax.fori_loop(0, atoms // group, some_atoms, 0)
 
     @pl.when(step == pl.num_programs(0) - 1)
@@ -357,7 +363,7 @@
             jnp.dot(high, w_out[...], preferred_element_type=jnp.float32)
             + jnp.dot(low_part, w_out[...], preferred_element_type=jnp.float32)
         ) * (1.0 / math.sqrt(degree))
-        out_ref[...] = jnp.where(live(channels), aggregate + spread_t.T * scale, 0.0)
+        out_ref[...] = aggregate + spread_t.T * scale
 
 
 def whole(shape):
@@ -379,7 +385,7 @@
         grid=(atom_rows // step,),
         in_specs=[
             pl.BlockSpec((step * degree,), lambda i: (i,), memory_space=pltpu.SMEM),
-            pl.BlockSpec((edge_basis.shape[0], step * degree), lambda i: (0, i)),
+            whole(edge_basis.shape),
             whole(features.shape),
             pl.BlockSpec(memory_space=pltpu.SMEM),
             whole(base_cos.shape),
@@ -392,7 +398,7 @@
         out_shape=jax.ShapeDtypeStruct((atom_rows, channels), f32),
         scratch_shapes=[
             pltpu.VMEM((3, blocks, atom_rows, channels), bf16),
-            pltpu.VMEM((3 * blocks * atom_rows, 8, channels), f32),
+            pltpu.VMEM((3 * blocks * atom_rows, channels), f32),
             pltpu.VMEM((atom_rows, channels), bf16),
             pltpu.VMEM((PAIRS, atom_rows), f32),
             pltpu.VMEM((PAIRS, atom_rows), f32),
@@ -400,6 +406,7 @@
             pltpu.VMEM((grid_rows, 2 * channels), bf16),
             pltpu.VMEM((2 * grid_rows, channels), f32),
             pltpu.VMEM((atom_rows, channels), f32),
+            pltpu.VMEM((atom_rows * degree, channels), f32),
             pltpu.VMEM((atom_rows, channels), f32),
             pltpu.VMEM((members - 1, lines * share, 2 * channels), bf16),
             pltpu.VMEM((lines * share, 2 * channels), f32),
@@ -474,7 +481,7 @@
     filter_rows = jnp.concatenate([filter_sum, filter_sum])
     plan = (degree, cols, low, members, lines, share, norm_factor, 4.0 / math.sqrt(total_k))
     weights = (w_send, w_recv, w_basis, w_out)
-    return force_step(
+    unmasked = force_step(
         features,
         atom_count,
         senders,
@@ -486,6 +493,8 @@
         w_mix,
         plan,
     )
+    live = jnp.arange(atom_rows, dtype=jnp.int32) < atom_count[0]
+    return jnp.where(live[:, None], unmasked, 0.0)
 
 
 def solution(mesh):

time: 80.7 us -> 98.8 us (1.22)
  the two profiles are of different devices: /device:TPU:1 before, /device:TPU:0 now
where the time goes in v3:
time: 98.8 us; the launch traced here: 98.5 us
  Pallas kernels  90.9 us (92%)
  other arithmetic  5.18 us (5%)
  local copies, waits for them, and re-layouts  1.21 us (1%)
    pallas_call x1, Pallas kernels, force_step(): pl.pallas_call(lambda *refs: fused_kernel(plan, *refs), grid=(atom_rows /...  90.9 us
    select_n x1, other arithmetic, per_device(): return jnp.where(live[:, None], unmasked, 0.0)  2.04 us

profile of v3, /device:TPU:0, one launch (start us, length us, event | category | flops | bytes accessed | tf_op | source)
XLA Modules:
  0.0 98.5 jit_solution(16302116727507225773)
XLA Ops:
  0.0 0.0 copy-start
  0.0 0.0 copy-start.2
  0.0 0.8 copy-done.2
  0.9 0.4 copy-done
  1.2 0.5 fusion
  1.8 0.0 copy-start.3
  1.8 0.6 pad_maximum_fusion.refs_10_
  2.4 0.1 pad_maximum_fusion.1
  2.5 0.0 copy-done.3
  2.5 0.0 copy-start.1
  2.5 1.5 %fusion.3 = (f32[48,1024]{1,0:T(8,128)}, f32[48,1024]{1,0:T(8,128)}) fusion(f32[3,1024]{1,0:T(4,128)S(1)} %copy-done.3, f32[48]{0:T(128)S(1)} %pad_maximum_fusion.1), kind=kLoop, calls=%fused_computation.6 | loop fusion | flops 196608 | bytes 405696 | tf_op jit(solution)/shard_map/sin | solution.py:490
  4.7 0.0 copy-done.1
  4.7 0.9 subtract_add_fusion.refs_0_
  5.5 90.9 %force_step.1 = f32[1024,128]{1,0:T(8,128)} custom-call(s32[32768]{0:T(1024)} %subtract_add_fusion.refs_0_, bf16[8,32768]{1,0:T(8,128)(2,1)} %refs_1_.1, bf16[1024,128]{1,0:T(8,128)(2,1)} %refs_2_.1, s32[1]{0:T(128)} %copy.13.refs_3_, f32[48,1024]{1,0:T(8,128)} %get-tuple-element.6.refs_4_, f32[48,1024]{1,0:T(8,128)} %get-tuple-element.5.refs_5_, ...), custom_call_target="tpu_custom_call" | custom-call | flops 838860800 | bytes 67108864 | tf_op jit(solution)/shard_map/force_step/pallas_call | solution.py:383
  96.5 2.0 %broadcast_select_fusion = f32[1024,128]{1,0:T(8,128)} fusion(f32[1024,128]{1,0:T(8,128)} %force_step.1, pred[1024]{0:T(1024)(128)(4,1)S(1)} %iota_compare_fusion), kind=kLoop, calls=%fused_computation.3 | loop fusion | flops 131072 | bytes 1049600 | tf_op jit(solution)/shard_map/jit(_where)/select_n | solution.py:497
  (5 shorter events, 0.1 us)
Async XLA Ops:
  0.0 1.2 %copy-start = (f32[2048,128]{1,0:T(8,128)S(1)}, f32[2048,128]{1,0:T(8,128)}, u32[]{:S(2)}) copy-start(f32[2048,128]{1,0:T(8,128)} %param.16) | copy-start | bytes 3145732
  0.0 0.8 copy-start.2
  1.8 0.7 copy-start.3
  2.5 2.2 %copy-start.1 = (s32[32768]{0:T(1024)S(1)}, s32[32768]{0:T(1024)}, u32[]{:S(2)}) copy-start(s32[32768]{0:T(1024)} %param.23) | copy-start | bytes 393220

commit v4 on v3

--- a/solution.py
+++ b/solution.py
@@ -50,21 +50,44 @@
         sums_ref[SIDE * PAIRS :, :] = jnp.zeros((tail, 2 * channels), jnp.bfloat16)
 
 
-def edge_rows(degree, group, it, snd_ref, pool, base, total):
+def edge_loop(degree, snd_ref, pool, base, base_first, total, total_first):
+    group = 4
     edges = group * degree
-    first = pl.multiple_of(it * edges, edges)
-    row = pl.multiple_of(it * group, group)
-    sums = []
-    for j in range(group):
-        at = first + j * degree
-        rows = [pool[pl.ds(snd_ref[at + e], 1), :] for e in range(degree)]
-        half = jnp.concatenate(rows, axis=0) + base[pl.ds(pl.multiple_of(at, degree), degree), :]
-        hidden = (half + half * jnp.tanh(half)).astype(jnp.bfloat16)
-        sums.append(jnp.sum(hidden.astype(jnp.float32), axis=0, keepdims=True))
-    total[pl.ds(row, group), :] = jnp.concatenate(sums, axis=0)
-
-
-def edge_base(degree, basis_ref, w_basis, recv, base):
+    count = snd_ref.shape[0] // edges
+    sublane = lax.broadcasted_iota(jnp.int32, pool.shape[1:], 0)
+    masks = [sublane == k for k in range(8)]
+
+    def gather(it):
+        first = pl.multiple_of(it * edges, edges)
+        parts = []
+        for octet in range(edges // 8):
+            start = first + octet * 8
+            picked = pool[snd_ref[start]]
+            for k in range(1, 8):
+                picked = jnp.where(masks[k], pool[snd_ref[start + k]], picked)
+            at = pl.multiple_of(base_first + first + octet * 8, 8)
+            parts.append(picked + base[pl.ds(at, 8), :])
+        return tuple(parts)
+
+    def finish(it, halves):
+        row = total_first + it * group
+        for j in range(group):
+            acc = None
+            for half in halves[j * degree // 8 : (j + 1) * degree // 8]:
+                hidden = (half + half * jnp.tanh(half)).astype(jnp.bfloat16).astype(jnp.float32)
+                acc = hidden if acc is None else acc + hidden
+            total[pl.ds(row + j, 1), :] = jnp.sum(acc, axis=0, keepdims=True)
+
+    def one(it, halves):
+        following = gather(it + 1)
+        finish(it, halves)
+        return following
+
+    last = lax.fori_loop(0, count - 1, one, gather(0))
+    finish(count - 1, last)
+
+
+def edge_base(degree, basis_ref, w_basis, recv, base, start, count):
     atoms = 8
     edges = atoms * degree
     channels = recv.shape[1]
@@ -72,17 +95,17 @@
     def some(n, carry):
         first = pl.multiple_of(n * edges, edges)
         radial = lax.dot_general(
-            basis_ref[:, pl.ds(first, edges)],
+            basis_ref[:, pl.ds(pl.multiple_of(start * degree + first, edges), edges)],
             w_basis[...],
             CONTRACT_FIRST,
             preferred_element_type=jnp.float32,
         )
-        rows = recv[pl.ds(pl.multiple_of(n * atoms, atoms), atoms), :]
+        rows = recv[pl.ds(pl.multiple_of(start + n * atoms, atoms), atoms), :]
         both = radial.reshape(atoms, degree, channels) + rows[:, None, :]
         base[pl.ds(first, edges), :] = 0.5 * both.reshape(edges, channels)
         return carry
 
-    lax.fori_loop(0, recv.shape[0] // atoms, some, 0)
+    lax.fori_loop(0, count // atoms, some, 0)
 
 
 def fused_kernel(
@@ -134,6 +157,8 @@
     slabs = low * lines
     home = 0 if cols == 2 else 1
     blocks = strips.shape[1]
+    atoms = snd_ref.shape[0] // degree
+    whole_base = base.shape[0] == block_rows * degree
     step = pl.program_id(0)
     slab, sub = lax.axis_index("slab"), lax.axis_index("sub")
     line = slab // low
@@ -236,7 +261,9 @@
         def some(n, carry):
             at = pl.multiple_of(n * 16, 16)
             rows = strips[a, c, pl.ds(at, 16), :].astype(jnp.float32)
-            pool[pl.ds(pl.multiple_of(first + at, 16), 16), :] = 0.5 * rows
+            pool[pl.ds(first + at, 16)] = jnp.broadcast_to(
+                (0.5 * rows)[:, None, :], (16, 8, channels)
+            )
             return carry
 
         lax.fori_loop(0, block_rows // 16, some, 0)
@@ -276,17 +303,19 @@
             copy_x(n).wait_recv()
             for up in (1, 0):
                 copy_z(up, slot).start()
-        each(members, lambda r: copy_a(r).start())
         recv[...] = jnp.dot(feat_ref[...], w_recv[...], preferred_element_type=jnp.float32)
-        edge_base(degree, basis_ref, w_basis, recv, base)
+        if whole_base:
+            edge_base(degree, basis_ref, w_basis, recv, base, 0, block_rows)
         for c in range(blocks):
             spread(1, c)
         for c in [home] + [slot for by, slot in sides]:
             for up in (1, 0):
                 copy_z(up, c).wait_recv()
+                if c == sides[-1][1] and up == 0:
+                    each(members, lambda r: copy_a(r).start())
                 spread(0 if up else 2, c)
 
-    @pl.when(step == 3)
+    @pl.when(step == 2)
     def _():
         each(members, lambda r: copy_a(r).wait_recv())
         part[...] = sums_ref[pl.ds(pl.multiple_of(member * chunk, 16), chunk), :].astype(jnp.float32)
@@ -297,7 +326,7 @@
         each(members, add)
         each(lines, lambda r: copy_b(r).start())
 
-    @pl.when(step == 6)
+    @pl.when(step == 4)
     def _():
         each(lines, lambda r: copy_b(r).wait_recv())
         owned = part[pl.ds(pl.multiple_of(line * share, 8), share), :]
@@ -313,22 +342,15 @@
         ).astype(jnp.bfloat16)
         each(lines, lambda r: copy_c(r).start())
 
-    @pl.when(step == 9)
+    @pl.when(step == 5)
     def _():
         each(lines, lambda r: copy_c(r).wait_recv())
         each(members, lambda r: copy_d(r).start())
 
-    atoms = snd_ref.shape[0] // degree
-    group = 16
-
-    def some_atoms(it, carry):
-        edge_rows(degree, group, it, snd_ref, pool, base_now, total_now)
-        return carry
-
-    here = pl.ds(pl.multiple_of(step * atoms, atoms), atoms)
-    total_now = total.at[here]
-    base_now = base.at[pl.ds(pl.multiple_of(step * atoms * degree, atoms * degree), atoms * degree)]
-    lax.fori_loop(0, atoms // group, some_atoms, 0)
+    row = pl.multiple_of(step * atoms, atoms)
+    if not whole_base:
+        edge_base(degree, basis_ref, w_basis, recv, base, row, atoms)
+    edge_loop(degree, snd_ref, pool, base, row * degree if whole_base else 0, total, row)
 
     @pl.when(step == pl.num_programs(0) - 1)
     def _():
@@ -377,7 +399,8 @@
     atom_rows, channels = features.shape
     grid_rows = members * lines * share
     blocks = 2 if cols == 2 else 3
-    step = 64
+    step = 128
+    base_atoms = atom_rows if cols == 2 else step
     dma = pltpu.SemaphoreType.DMA
     f32, bf16 = jnp.float32, jnp.bfloat16
     return pl.pallas_call(
@@ -398,7 +421,7 @@
         out_shape=jax.ShapeDtypeStruct((atom_rows, channels), f32),
         scratch_shapes=[
             pltpu.VMEM((3, blocks, atom_rows, channels), bf16),
-            pltpu.VMEM((3 * blocks * atom_rows, channels), f32),
+            pltpu.VMEM((3 * blocks * atom_rows, 8, channels), f32),
             pltpu.VMEM((atom_rows, channels), bf16),
             pltpu.VMEM((PAIRS, atom_rows), f32),
             pltpu.VMEM((PAIRS, atom_rows), f32),
@@ -406,7 +429,7 @@
             pltpu.VMEM((grid_rows, 2 * channels), bf16),
             pltpu.VMEM((2 * grid_rows, channels), f32),
             pltpu.VMEM((atom_rows, channels), f32),
-            pltpu.VMEM((atom_rows * degree, channels), f32),
+            pltpu.VMEM((base_atoms * degree, channels), f32),
             pltpu.VMEM((atom_rows, channels), f32),
             pltpu.VMEM((members - 1, lines * share, 2 * channels), bf16),
             pltpu.VMEM((lines * share, 2 * channels), f32),

time: 98.8 us -> 94.9 us (0.961)
  Pallas kernels: 90.9 us -> 86.9 us
    pallas_call x1, Pallas kernels: 90.9 us -> 86.9 us  [force_step(): pl.pallas_call(lambda *refs: fused_kernel(plan, *refs), grid=(atom_rows /...]
where the time goes in v4:
time: 94.9 us; the launch traced here: 94.5 us
  Pallas kernels  86.9 us (92%)
  other arithmetic  5.18 us (5%)
  local copies, waits for them, and re-layouts  1.21 us (1%)
    pallas_call x1, Pallas kernels, force_step(): pl.pallas_call(lambda *refs: fused_kernel(plan, *refs), grid=(atom_rows /...  86.9 us
    select_n x1, other arithmetic, per_device(): return jnp.where(live[:, None], unmasked, 0.0)  2.04 us

profile of v4, /device:TPU:0, one launch (start us, length us, event | category | flops | bytes accessed | tf_op | source)
XLA Modules:
  0.0 94.5 jit_solution(10745567687238796606)
XLA Ops:
  0.0 0.0 copy-start
  0.0 0.0 copy-start.2
  0.0 0.8 copy-done.2
  0.9 0.4 copy-done
  1.2 0.5 fusion
  1.8 0.0 copy-start.3
  1.8 0.6 pad_maximum_fusion.refs_10_
  2.4 0.1 pad_maximum_fusion.1
  2.5 0.0 copy-done.3
  2.5 0.0 copy-start.1
  2.5 1.5 %fusion.3 = (f32[48,1024]{1,0:T(8,128)}, f32[48,1024]{1,0:T(8,128)}) fusion(f32[3,1024]{1,0:T(4,128)S(1)} %copy-done.3, f32[48]{0:T(128)S(1)} %pad_maximum_fusion.1), kind=kLoop, calls=%fused_computation.6 | loop fusion | flops 196608 | bytes 405696 | tf_op jit(solution)/shard_map/sin | solution.py:513
  4.7 0.0 copy-done.1
  4.7 0.9 subtract_add_fusion.refs_0_
  5.5 86.9 %force_step.1 = f32[1024,128]{1,0:T(8,128)} custom-call(s32[32768]{0:T(1024)} %subtract_add_fusion.refs_0_, bf16[8,32768]{1,0:T(8,128)(2,1)} %refs_1_.1, bf16[1024,128]{1,0:T(8,128)(2,1)} %refs_2_.1, s32[1]{0:T(128)} %copy.13.refs_3_, f32[48,1024]{1,0:T(8,128)} %get-tuple-element.6.refs_4_, f32[48,1024]{1,0:T(8,128)} %get-tuple-element.5.refs_5_, ...), custom_call_target="tpu_custom_call" | custom-call | flops 838860800 | bytes 67108864 | tf_op jit(solution)/shard_map/force_step/pallas_call | solution.py:406
  92.5 2.0 %broadcast_select_fusion = f32[1024,128]{1,0:T(8,128)} fusion(f32[1024,128]{1,0:T(8,128)} %force_step.1, pred[1024]{0:T(1024)(128)(4,1)S(1)} %iota_compare_fusion), kind=kLoop, calls=%fused_computation.3 | loop fusion | flops 131072 | bytes 1049600 | tf_op jit(solution)/shard_map/jit(_where)/select_n | solution.py:520
  (5 shorter events, 0.1 us)
Async XLA Ops:
  0.0 1.2 %copy-start = (f32[2048,128]{1,0:T(8,128)S(1)}, f32[2048,128]{1,0:T(8,128)}, u32[]{:S(2)}) copy-start(f32[2048,128]{1,0:T(8,128)} %param.16) | copy-start | bytes 3145732
  0.0 0.8 copy-start.2
  1.8 0.7 copy-start.3
  2.5 2.2 %copy-start.1 = (s32[32768]{0:T(1024)S(1)}, s32[32768]{0:T(1024)}, u32[]{:S(2)}) copy-start(s32[32768]{0:T(1024)} %param.23) | copy-start | bytes 393220

commit v5 on v4

--- a/solution.py
+++ b/solution.py
@@ -54,7 +54,7 @@
     group = 4
     edges = group * degree
     count = snd_ref.shape[0] // edges
-    sublane = lax.broadcasted_iota(jnp.int32, pool.shape[1:], 0)
+    sublane = lax.broadcasted_iota(jnp.int32, (8, pool.shape[1]), 0)
     masks = [sublane == k for k in range(8)]
 
     def gather(it):
@@ -62,9 +62,9 @@
         parts = []
         for octet in range(edges // 8):
             start = first + octet * 8
-            picked = pool[snd_ref[start]]
+            picked = pool[pl.ds(snd_ref[start], 8), :]
             for k in range(1, 8):
-                picked = jnp.where(masks[k], pool[snd_ref[start + k]], picked)
+                picked = jnp.where(masks[k], pool[pl.ds(snd_ref[start + k], 8), :], picked)
             at = pl.multiple_of(base_first + first + octet * 8, 8)
             parts.append(picked + base[pl.ds(at, 8), :])
         return tuple(parts)
@@ -88,7 +88,7 @@
 
 
 def edge_base(degree, basis_ref, w_basis, recv, base, start, count):
-    atoms = 8
+    atoms = 64
     edges = atoms * degree
     channels = recv.shape[1]
 
@@ -261,9 +261,7 @@
         def some(n, carry):
             at = pl.multiple_of(n * 16, 16)
             rows = strips[a, c, pl.ds(at, 16), :].astype(jnp.float32)
-            pool[pl.ds(first + at, 16)] = jnp.broadcast_to(
-                (0.5 * rows)[:, None, :], (16, 8, channels)
-            )
+            pool[pl.ds(pl.multiple_of(first + at + 8, 8), 16), :] = 0.5 * rows
             return carry
 
         lax.fori_loop(0, block_rows // 16, some, 0)
@@ -274,6 +272,9 @@
 
     @pl.when(step == 0)
     def _():
+        margin = jnp.zeros((8, channels), jnp.float32)
+        pool[:8, :] = margin
+        pool[pool.shape[0] - 8 :, :] = margin
         strips[1, home] = jnp.dot(
             feat_ref[...], w_send[...], preferred_element_type=jnp.float32
         ).astype(jnp.bfloat16)
@@ -400,7 +401,7 @@
     grid_rows = members * lines * share
     blocks = 2 if cols == 2 else 3
     step = 128
-    base_atoms = atom_rows if cols == 2 else step
+    base_atoms = atom_rows
     dma = pltpu.SemaphoreType.DMA
     f32, bf16 = jnp.float32, jnp.bfloat16
     return pl.pallas_call(
@@ -421,7 +422,7 @@
         out_shape=jax.ShapeDtypeStruct((atom_rows, channels), f32),
         scratch_shapes=[
             pltpu.VMEM((3, blocks, atom_rows, channels), bf16),
-            pltpu.VMEM((3 * blocks * atom_rows, 8, channels), f32),
+            pltpu.VMEM((3 * blocks * atom_rows + 16, channels), f32),
             pltpu.VMEM((atom_rows, channels), bf16),
             pltpu.VMEM((PAIRS, atom_rows), f32),
             pltpu.VMEM((PAIRS, atom_rows), f32),
@@ -484,6 +485,8 @@
         slab_step = block // 3
         col_step = block - 3 * slab_step
         senders = (slab_step * 2 + (col_step != 1)) * atom_rows + (senders - block * atom_rows)
+
+    senders = senders + (8 - jnp.arange(senders.shape[0], dtype=jnp.int32) % 8)
 
     steps = jnp.arange(16, dtype=jnp.float32)
     waves = jnp.concatenate([steps, steps - KMAX, steps - KMAX])

time: 94.9 us -> 63.6 us (0.67)
  Pallas kernels: 86.9 us -> 55.7 us
    pallas_call x1, Pallas kernels: 86.9 us -> 55.7 us  [force_step(): pl.pallas_call(lambda *refs: fused_kernel(plan, *refs), grid=(atom_rows /...]
where the time goes in v5:
time: 63.6 us; the launch traced here: 63.3 us
  Pallas kernels  55.7 us (88%)
  other arithmetic  5.2 us (8%)
  local copies, waits for them, and re-layouts  1.21 us (2%)
  between operations  0.7 us (1%)
    pallas_call x1, Pallas kernels, force_step(): pl.pallas_call(lambda *refs: fused_kernel(plan, *refs), grid=(atom_rows /...  55.7 us
    select_n x1, other arithmetic, per_device(): return jnp.where(live[:, None], unmasked, 0.0)  2.04 us
    sin x1, other arithmetic, per_device(): jnp.sin(angles)  1.52 us

profile of v5, /device:TPU:0, one launch (start us, length us, event | category | flops | bytes accessed | tf_op | source)
XLA Modules:
  0.0 63.3 jit_solution(18093138956126534795)
XLA Ops:
  0.0 0.0 copy-start
  0.0 0.0 copy-start.2
  0.0 0.8 %copy-done.2 = s32[3,2048]{1,0:T(4,128)S(1)} copy-done((s32[3,2048]{1,0:T(4,128)S(1)}, s32[3,2048]{1,0:T(4,128)}, u32[]{:S(2)}) %copy-start.2) | copy-done | bytes 24600
  0.9 0.4 copy-done
  1.2 0.5 fusion
  1.8 0.0 copy-start.3
  1.8 0.6 pad_maximum_fusion.refs_10_
  2.4 0.1 pad_maximum_fusion.1
  2.5 0.0 copy-done.3
  2.5 0.0 copy-start.1
  2.5 1.5 %fusion.3 = (f32[48,1024]{1,0:T(8,128)}, f32[48,1024]{1,0:T(8,128)}) fusion(f32[3,1024]{1,0:T(4,128)S(1)} %copy-done.3, f32[48]{0:T(128)S(1)} %pad_maximum_fusion.1), kind=kLoop, calls=%fused_computation.6 | loop fusion | flops 196608 | bytes 405696 | tf_op jit(solution)/shard_map/sin | solution.py:516
  4.7 0.0 copy-done.1
  4.7 0.9 %fusion.9.refs_0_ = s32[32768]{0:T(1024)} fusion(s32[32768]{0:T(1024)S(1)} %copy-done.1), kind=kLoop, calls=%fused_computation.18 | loop fusion | flops 1343488 | bytes 262144 | tf_op jit(solution)/shard_map/add | solution.py:489
  5.6 55.7 %force_step.1 = f32[1024,128]{1,0:T(8,128)} custom-call(s32[32768]{0:T(1024)} %fusion.9.refs_0_, bf16[8,32768]{1,0:T(8,128)(2,1)} %refs_1_.1, bf16[1024,128]{1,0:T(8,128)(2,1)} %refs_2_.1, s32[1]{0:T(128)} %copy.13.refs_3_, f32[48,1024]{1,0:T(8,128)} %get-tuple-element.6.refs_4_, f32[48,1024]{1,0:T(8,128)} %get-tuple-element.5.refs_5_, ...), custom_call_target="tpu_custom_call" | custom-call | flops 838860800 | bytes 67108864 | tf_op jit(solution)/shard_map/force_step/pallas_call | solution.py:407
  61.3 2.0 %broadcast_select_fusion = f32[1024,128]{1,0:T(8,128)} fusion(f32[1024,128]{1,0:T(8,128)} %force_step.1, pred[1024]{0:T(1024)(128)(4,1)S(1)} %iota_compare_fusion), kind=kLoop, calls=%fused_computation.3 | loop fusion | flops 131072 | bytes 1049600 | tf_op jit(solution)/shard_map/jit(_where)/select_n | solution.py:523
  (5 shorter events, 0.1 us)
Async XLA Ops:
  0.0 1.2 %copy-start = (f32[2048,128]{1,0:T(8,128)S(1)}, f32[2048,128]{1,0:T(8,128)}, u32[]{:S(2)}) copy-start(f32[2048,128]{1,0:T(8,128)} %param.16) | copy-start | bytes 3145732
  0.0 0.8 %copy-start.2 = (s32[3,2048]{1,0:T(4,128)S(1)}, s32[3,2048]{1,0:T(4,128)}, u32[]{:S(2)}) copy-start(s32[3,2048]{1,0:T(4,128)} %param.15) | copy-start | bytes 73732
  1.8 0.7 %copy-start.3 = (f32[3,1024]{1,0:T(4,128)S(1)}, f32[3,1024]{1,0:T(4,128)}, u32[]{:S(2)}) copy-start(f32[3,1024]{1,0:T(4,128)} %param.13) | copy-start | bytes 36868
  2.5 2.2 %copy-start.1 = (s32[32768]{0:T(1024)S(1)}, s32[32768]{0:T(1024)}, u32[]{:S(2)}) copy-start(s32[32768]{0:T(1024)} %param.23) | copy-start | bytes 393220

commit v6 on v5

--- a/solution.py
+++ b/solution.py
@@ -12,6 +12,37 @@
 PAIRS = 96
 MIB = 1024 * 1024
 CONTRACT_FIRST = (((0,), (0,)), ((), ()))
+
+
+def fill_base(positions, base_cos, base_sin):
+    rows = lax.broadcasted_iota(jnp.int32, (16, positions.shape[1]), 0).astype(jnp.float32)
+    for axis in range(3):
+        turns = (rows if axis == 0 else rows - KMAX) * positions[axis : axis + 1, :]
+        angle = (turns - jnp.round(turns)) * math.pi
+        square = angle * angle
+        sine = jnp.full_like(angle, -1.0 / math.factorial(11))
+        for n, sign in ((9, 1), (7, -1), (5, 1), (3, -1), (1, 1)):
+            sine = sine * square + sign / math.factorial(n)
+        sine = sine * angle
+        cosine = jnp.full_like(angle, 1.0 / math.factorial(12))
+        for n, sign in ((10, -1), (8, 1), (6, -1), (4, 1), (2, -1), (0, 1)):
+            cosine = cosine * square + sign / math.factorial(n)
+        base_cos[axis * 16 : axis * 16 + 16, :] = 1.0 - 2.0 * sine * sine
+        base_sin[axis * 16 : axis * 16 + 16, :] = 2.0 * sine * cosine
+
+
+def pick_filters(kgrid_ref, k_filter, first_row, share, filter_ref):
+    total_k = kgrid_ref.shape[1]
+    waves = [kgrid_ref[axis : axis + 1, :] for axis in range(3)]
+    flip = jnp.where(waves[0] < 0, -1, 1)
+    spot = (waves[2] * flip + KMAX) * PAIRS + waves[0] * flip * SIDE + waves[1] * flip + KMAX
+    rows = first_row + lax.broadcasted_iota(jnp.int32, (share, total_k), 0)
+    picks = jnp.where(rows == spot, 1.0, 0.0)
+    summed = jnp.dot(
+        picks, k_filter[...], precision=lax.Precision.HIGHEST, preferred_element_type=jnp.float32
+    )
+    filter_ref[:share, :] = summed
+    filter_ref[share:, :] = summed
 
 
 def fill_tables(base_cos, base_sin, masked_ref, table_ref, sums_ref, pair_cos, pair_sin):
@@ -114,15 +145,18 @@
     basis_ref,
     feat_ref,
     count_ref,
-    base_cos,
-    base_sin,
+    positions,
+    kgrid_ref,
+    k_filter,
     w_send,
     w_recv,
     w_basis,
     w_out,
-    filter_ref,
     w_mix,
     out_ref,
+    base_cos,
+    base_sin,
+    filter_ref,
     strips,
     pool,
     masked,
@@ -299,11 +333,13 @@
         masked[...] = jnp.where(live(channels), feat_ref[...].astype(jnp.float32), 0.0).astype(
             jnp.bfloat16
         )
+        fill_base(positions, base_cos, base_sin)
         fill_tables(base_cos, base_sin, masked, table, sums_ref, pair_cos, pair_sin)
         for n, (by, slot) in enumerate(sides):
             copy_x(n).wait_recv()
             for up in (1, 0):
                 copy_z(up, slot).start()
+        pick_filters(kgrid_ref, k_filter, (member * lines + line) * share, share, filter_ref)
         recv[...] = jnp.dot(feat_ref[...], w_recv[...], preferred_element_type=jnp.float32)
         if whole_base:
             edge_base(degree, basis_ref, w_basis, recv, base, 0, block_rows)
@@ -394,7 +430,7 @@
 
 
 def force_step(
-    features, atom_count, senders, edge_basis, base_cos, base_sin, weights, filter_rows, w_mix, plan
+    features, atom_count, senders, edge_basis, positions, kgrid, k_filter, weights, w_mix, plan
 ):
     degree, cols, low, members, lines, share, norm_factor, scale = plan
     atom_rows, channels = features.shape
@@ -412,15 +448,18 @@
             whole(edge_basis.shape),
             whole(features.shape),
             pl.BlockSpec(memory_space=pltpu.SMEM),
-            whole(base_cos.shape),
-            whole(base_sin.shape),
+            whole(positions.shape),
+            whole(kgrid.shape),
+            whole(k_filter.shape),
             *[whole(weight.shape) for weight in weights],
-            whole(filter_rows.shape),
             whole(w_mix.shape),
         ],
         out_specs=whole((atom_rows, channels)),
         out_shape=jax.ShapeDtypeStruct((atom_rows, channels), f32),
         scratch_shapes=[
+            pltpu.VMEM((48, atom_rows), f32),
+            pltpu.VMEM((48, atom_rows), f32),
+            pltpu.VMEM((2 * share, channels), f32),
             pltpu.VMEM((3, blocks, atom_rows, channels), bf16),
             pltpu.VMEM((3 * blocks * atom_rows + 16, channels), f32),
             pltpu.VMEM((atom_rows, channels), bf16),
@@ -453,7 +492,7 @@
         ),
         name="force_step",
     )(
-        senders, edge_basis, features, atom_count, base_cos, base_sin, *weights, filter_rows, w_mix
+        senders, edge_basis, features, atom_count, positions, kgrid, k_filter, *weights, w_mix
     )
 
 
@@ -488,23 +527,9 @@
 
     senders = senders + (8 - jnp.arange(senders.shape[0], dtype=jnp.int32) % 8)
 
-    steps = jnp.arange(16, dtype=jnp.float32)
-    waves = jnp.concatenate([steps, steps - KMAX, steps - KMAX])
-    turns = waves[:, None] * jnp.repeat(positions, 16, axis=0)
-    angles = (turns - jnp.round(turns)) * (2.0 * math.pi)
     low = 4
     lines = lax.axis_size("slab") // low
     members = low * cols
-    slab, sub = lax.axis_index("slab"), lax.axis_index("sub")
-    piece = ((slab % low) * cols + sub) * lines + slab // low
-    flip = jnp.where(kgrid[0] < 0, -1, 1)
-    grid_of_k = (kgrid[2] * flip + KMAX) * PAIRS + kgrid[0] * flip * SIDE + kgrid[1] * flip + KMAX
-    my_rows = piece * share + jnp.arange(share, dtype=jnp.int32)
-    picks = (my_rows[:, None] == grid_of_k[None, :]).astype(jnp.float32)
-    filter_sum = jnp.dot(
-        picks, k_filter, precision=lax.Precision.HIGHEST, preferred_element_type=jnp.float32
-    )
-    filter_rows = jnp.concatenate([filter_sum, filter_sum])
     plan = (degree, cols, low, members, lines, share, norm_factor, 4.0 / math.sqrt(total_k))
     weights = (w_send, w_recv, w_basis, w_out)
     unmasked = force_step(
@@ -512,10 +537,10 @@
         atom_count,
         senders,
         edge_basis,
-        jnp.cos(angles),
-        jnp.sin(angles),
+        positions,
+        kgrid,
+        k_filter,
         weights,
-        filter_rows,
         w_mix,
         plan,
     )

time: 63.6 us -> 61.3 us (0.964)
  other arithmetic: 5.2 us -> 3.83 us
  local copies, waits for them, and re-layouts: 1.21 us -> 0 us
  Pallas kernels: 55.7 us -> 56.6 us
    sin x1 -> x0, other arithmetic: 1.52 us -> none  [per_device(): jnp.sin(angles)]
    unnamed x8 -> x0, local copies, waits for them, and re-layouts: 1.21 us -> none
    pallas_call x1, Pallas kernels: 55.7 us -> 56.6 us  [force_step(): pl.pallas_call(lambda *refs: fused_kernel(plan, *refs), grid=(atom_rows /...]
    add x1, other arithmetic: 0.89 us -> 1.78 us  [per_device(): senders = senders + (8 - jnp.arange(senders.shape[0], dtype=jnp.int32) % 8)]
    concatenate x2 -> x0, other arithmetic: 0.7 us -> none  [the longest x1 0.62 us: per_device(): filter_rows = jnp.concatenate([filter_sum, filter_sum])]
where the time goes in v6:
time: 61.3 us; the launch traced here: 61.1 us
  Pallas kernels  56.6 us (92%)
  other arithmetic  3.83 us (6%)
  between operations  0.67 us (1%)
    pallas_call x1, Pallas kernels, force_step(): pl.pallas_call(lambda *refs: fused_kernel(plan, *refs), grid=(atom_rows /...  56.6 us
    select_n x1, other arithmetic, per_device(): return jnp.where(live[:, None], unmasked, 0.0)  2.04 us
    add x1, other arithmetic, per_device(): senders = senders + (8 - jnp.arange(senders.shape[0], dtype=jnp.int32) % 8)  1.78 us

profile of v6, /device:TPU:0, one launch (start us, length us, event | category | flops | bytes accessed | tf_op | source)
XLA Modules:
  0.0 61.1 jit_solution(16099523142456337046)
XLA Ops:
  0.7 1.8 %fusion.2.refs_0_ = s32[32768]{0:T(1024)} fusion(s32[32768]{0:T(1024)} %param.23), kind=kLoop, calls=%fused_computation.9 | loop fusion | flops 1343488 | bytes 262144 | tf_op jit(solution)/shard_map/add | solution.py:528
  2.4 56.6 %force_step.1 = f32[1024,128]{1,0:T(8,128)} custom-call(s32[32768]{0:T(1024)} %fusion.2.refs_0_, bf16[8,32768]{1,0:T(8,128)(2,1)} %refs_1_.1, bf16[1024,128]{1,0:T(8,128)(2,1)} %refs_2_.1, s32[1]{0:T(128)} %copy.13.refs_3_, f32[3,1024]{1,0:T(4,128)} %refs_4_.1, s32[3,2048]{1,0:T(4,128)} %refs_5_.1, f32[2048,128]{1,0:T(8,128)} %refs_6_.1, ...), custom_call_target="tpu_custom_call" | custom-call | flops 838860800 | bytes 67108864 | tf_op jit(solution)/shard_map/force_step/pallas_call | solution.py:443
  59.0 2.0 %broadcast_select_fusion = f32[1024,128]{1,0:T(8,128)} fusion(f32[1024,128]{1,0:T(8,128)} %force_step.1, pred[1024]{0:T(1024)(128)(4,1)S(1)} %iota_compare_fusion), kind=kLoop, calls=%fused_computation | loop fusion | flops 131072 | bytes 1049600 | tf_op jit(solution)/shard_map/jit(_where)/select_n | solution.py:548
  (1 shorter events, 0.0 us)
